TPU v7x, 128 devices: a whole 4x4x4 slice. The times are simulated.
128 devices in a mesh: dp: 8 (over x, core), mem: 16 (over z, y).
Axes of the slice: x: 4, y: 4, z: 4, core: 2. Of those that a mesh axis runs over, the one named last changes fastest.
Arguments:
- tokens: bfloat16 [256, 256, 1024], P(('dp', 'mem')), may hold values from -6 to 6
- memory: bfloat16 [256, 384, 1024], P('dp', 'mem'), may hold values from -6 to 6
- cotangent: bfloat16 [256, 256, 1024], P(('dp', 'mem')), may hold values from -24 to 24
- tgt_len: int32 [256], P(('dp', 'mem')), may hold values from 128 to 256, as said below
- src_len: int32 [256], P('dp'), may hold values from 24 to 384, as said below
- self_qkv: bfloat16 [1024, 3072], P('dp'), may hold values from -0.1875 to 0.1875
- self_out: bfloat16 [1024, 1024], P('dp'), may hold values from -0.75 to 0.75
- cross_q: bfloat16 [1024, 1024], P('dp'), may hold values from -0.1875 to 0.1875
- cross_kv: bfloat16 [1024, 2048], P('dp'), may hold values from -0.1875 to 0.1875
- cross_out: bfloat16 [1024, 1024], P('dp'), may hold values from -1 to 1
- ffn_in: bfloat16 [1024, 4096], P('dp'), may hold values from -0.1875 to 0.1875
- ffn_out: bfloat16 [4096, 1024], P('dp'), may hold values from -0.09375 to 0.09375
- first_gain: bfloat16 [1024], P('dp'), may hold values from 0.5 to 1.5
- first_bias: bfloat16 [1024], P('dp'), may hold values from -1 to 1
- second_gain: bfloat16 [1024], P('dp'), may hold values from 0.5 to 1.5
- second_bias: bfloat16 [1024], P('dp'), may hold values from -1 to 1
- third_gain: bfloat16 [1024], P('dp'), may hold values from 0.5 to 1.5
- third_bias: bfloat16 [1024], P('dp'), may hold values from -1 to 1
- prefix_key: bfloat16 [30, 1024], replicated, may hold values from -6 to 6
- prefix_value: bfloat16 [30, 1024], replicated, may hold values from -6 to 6
- down_weight: bfloat16 [1024, 512], replicated, may hold values from -0.1875 to 0.1875
- down_bias: bfloat16 [512], replicated, may hold values from -3 to 3
- up_weight: bfloat16 [512, 1024], replicated, may hold values from -0.0625 to 0.0625
- up_bias: bfloat16 [1024], replicated, may hold values from -0.59765625 to 0.59765625
Outputs:
- output: bfloat16 [256, 256, 1024], P(('dp', 'mem'))
- input_grad: bfloat16 [256, 256, 1024], P(('dp', 'mem'))
- memory_grad: bfloat16 [256, 384, 1024], P('dp', 'mem')
- keyprefix_grad: float32 [30, 1024], P(None, ('dp', 'mem'))
- valueprefix_grad: float32 [30, 1024], P(None, ('dp', 'mem'))
- downweight_grad: float32 [1024, 512], P(('dp', 'mem'))
- downbias_grad: float32 [512], P(('dp', 'mem'))
- upweight_grad: float32 [512, 1024], P(None, ('dp', 'mem'))
- upbias_grad: float32 [1024], P(('dp', 'mem'))
Inputs may be any that keep to these rules, and one draw needn't show every extreme that they name: `tgt_len`: sequences n with equal n // 32 and equal (n) % 2 form a group; each group holds one sequence of length 256 and another of half of 256. `src_len`: in each group as for tgt_len one sequence has 384 source positions and another has 24; short ones are more common.
All inputs are finite; a program needn't handle non-finite values.
Results may differ from a plain program's by a relative error of at most 0.023.
Values may be sent and summed in bfloat16 or wider, within the bound.
No kernel may reach another device: no remote copies, remote signals or barrier semaphores. Data moves between devices by JAX's collectives and lax.ppermute only.
A program may use at most 256 MiB of HBM per device.

v0:
```python
import functools

import jax
import jax.numpy as jnp
from jax import lax
from jax.experimental import pallas as pl
from jax.experimental.pallas import tpu as pltpu
from jax.sharding import Mesh
from jax.sharding import PartitionSpec as P

HEAD_DIM = 64
PAIR = 128
GROUP = 256
PREFIX = 30
PREFIX_PAD = 32
BIAS_ROWS = 4
MEM = ("mem_0", "mem_1")
DP = ("dp_0", "dp_1")
DP_MEM = ("dp_0", "dp_1", "mem_0", "mem_1")

NEGATIVE = -1e30
EPSILON = 1e-05
SCALE = HEAD_DIM ** (-0.5)
BF = jnp.bfloat16
F32 = jnp.float32
SPREAD = 4
STRIP = 128
FFN_BLOCK = 1024
FF_AT = 0
IN_AT = 4096
OUT_AT = 8192
SOUT_AT = 9216
CQ_AT = 10240
KV_AT = 11264
VMEM_BYTES = 60 * 1024 * 1024


def dot_nn(left, right):
    return lax.dot_general(left, right, (((1,), (0,)), ((), ())), preferred_element_type=F32)


def dot_nt(left, right):
    return lax.dot_general(left, right, (((1,), (1,)), ((), ())), preferred_element_type=F32)


def dot_tn(left, right):
    return lax.dot_general(left, right, (((0,), (0,)), ((), ())), preferred_element_type=F32)


def per_head(x):
    lane = lax.broadcasted_iota(jnp.int32, (1, GROUP), 1)
    return [
        x * jnp.where(lane // HEAD_DIM == h, 1.0, 0.0).astype(BF)
        for h in range(GROUP // HEAD_DIM)
    ]


def stacked(parts):
    return jnp.concatenate(parts, axis=0)


def beside(parts):
    return jnp.concatenate(parts, axis=1)


def cut(x, count, axis):
    size = x.shape[axis] // count
    return [lax.slice_in_dim(x, i * size, (i + 1) * size, axis=axis) for i in range(count)]


def norm_stats(hidden):
    centred = hidden - jnp.mean(hidden, axis=-1, keepdims=True)
    inverse = lax.rsqrt(jnp.mean(centred * centred, axis=-1, keepdims=True) + EPSILON)
    return centred * inverse, inverse


def norm_back(grad_in, normed, inverse, gain):
    scaled = grad_in * gain
    return inverse * (
        scaled
        - jnp.mean(scaled, axis=-1, keepdims=True)
        - normed * jnp.mean(scaled * normed, axis=-1, keepdims=True)
    )


def gelu_both(pre):
    cdf = 0.5 * (1.0 + lax.erf(pre * (0.5**0.5)))
    density = jnp.exp(-0.5 * pre * pre) * 0.3989422804014327
    return pre * cdf, cdf + pre * density


def self_forward_kernel(
    len_ref, tok_ref, wq_ref, wk_ref, wv_ref, pk_ref, pv_ref,
    q_ref, k_ref, v_ref, att_ref,
):
    seqs = len_ref.shape[0]
    rows_all = tok_ref.shape[0]
    tgt = rows_all // seqs
    projected = dot_nn(tok_ref[...], beside([wq_ref[...], wk_ref[...], wv_ref[...]])).astype(BF)
    q_ref[...] = projected[:, :GROUP]
    k_ref[...] = projected[:, GROUP : 2 * GROUP]
    v_ref[...] = projected[:, 2 * GROUP :]
    heads = GROUP // HEAD_DIM
    row = lax.broadcasted_iota(jnp.int32, (tgt, tgt), 0)
    col = lax.broadcasted_iota(jnp.int32, (tgt, tgt), 1)
    prefix_bias = jnp.where(
        lax.broadcasted_iota(jnp.int32, (1, PREFIX_PAD), 1) < PREFIX, 0.0, NEGATIVE
    )
    pk = per_head(pk_ref[...])
    pv = per_head(pv_ref[...])
    ones = stacked(
        per_head(jnp.ones((PREFIX_PAD, GROUP), BF)) + per_head(jnp.ones((tgt, GROUP), BF))
    )
    scores = []
    for s in range(seqs):
        here = pl.ds(s * tgt, tgt)
        scores.append(dot_nt(q_ref[here, :] * SCALE, stacked(pk + per_head(k_ref[here, :]))))
    for s in range(seqs):
        here = pl.ds(s * tgt, tgt)
        bias = jnp.where((col <= row) & (col < len_ref[s]), 0.0, NEGATIVE)
        pre = cut(scores[s][:, : heads * PREFIX_PAD], heads, 1)
        own = cut(scores[s][:, heads * PREFIX_PAD :], heads, 1)
        own_probs, pre_probs = [], []
        for x, y in zip(own, pre):
            x = x + bias
            y = y + prefix_bias
            top = jnp.maximum(jnp.max(x, axis=1, keepdims=True), jnp.max(y, axis=1, keepdims=True))
            own_probs.append(jnp.exp(x - top).astype(BF))
            pre_probs.append(jnp.exp(y - top).astype(BF))
        probs = beside(pre_probs + own_probs)
        total = dot_nn(probs, stacked(pv + per_head(v_ref[here, :])))
        att_ref[here, :] = (total / dot_nn(probs, ones)).astype(BF)


def cross_forward_kernel(
    len_ref, mem_ref, wk_ref, wv_ref, tok_ref, self_ref, wo_ref, wcq_ref, norm_ref,
    mk_ref, mv_ref, cq_ref, nrm1_ref, inv1_ref, att_ref,
):
    step = pl.program_id(0)
    seqs = len_ref.shape[0]
    tgt = tok_ref.shape[0] // seqs
    src = mem_ref.shape[0] // seqs

    @pl.when(step == 0)
    def _():
        for s in range(seqs):
            r = pl.ds(s * tgt, tgt)
            nrm, inv = norm_stats(
                tok_ref[r, :].astype(F32) + dot_nn(self_ref[r, :], wo_ref[...])
            )
            nrm1_ref[r, :] = nrm
            inv1_ref[r, :] = inv
            first = nrm * norm_ref[0:1, :] + norm_ref[1:2, :]
            cq_ref[r, :] = dot_nn(first.astype(BF), wcq_ref[...]).astype(BF)

    mem = mem_ref[...]
    projected = dot_nn(mem, beside([wk_ref[...], wv_ref[...]])).astype(BF)
    mk_ref[...] = projected[:, :GROUP]
    mv_ref[...] = projected[:, GROUP:]
    heads = GROUP // HEAD_DIM
    lanes = pl.ds(pl.multiple_of(step * GROUP, GROUP), GROUP)
    slot = lax.broadcasted_iota(jnp.int32, (1, src), 1)
    ones = stacked(per_head(jnp.ones((src, GROUP), BF)))
    scores = []
    for s in range(seqs):
        q = cq_ref[s * tgt : (s + 1) * tgt, lanes] * SCALE
        scores.append(dot_nt(q, stacked(per_head(mk_ref[s * src : (s + 1) * src, :]))))
    for s in range(seqs):
        bias = jnp.where(slot < len_ref[s], 0.0, NEGATIVE)
        probs = []
        for x in cut(scores[s], heads, 1):
            x = x + bias
            probs.append(jnp.exp(x - jnp.max(x, axis=1, keepdims=True)).astype(BF))
        probs = beside(probs)
        total = dot_nn(probs, stacked(per_head(mv_ref[s * src : (s + 1) * src, :])))
        att_ref[s * tgt : (s + 1) * tgt, :] = (total / dot_nn(probs, ones)).astype(BF)


def ffn_kernel(
    len_ref, nrm1_ref, att_ref, wco_ref, cot_ref, win_ref, wff_ref, down_ref, db_ref, up_ref, ub_ref,
    norm_ref,
    out_ref, gtwo_ref, adapt_ref,
    nrm2_ref, inv2_ref, acc_ref, low_ref, slope_ref, aact_ref, aslope_ref, g_ref,
    cot_here, down_here, up_here, out_here, adapt_here, sems,
):
    phase = pl.program_id(0)
    j = pl.program_id(1)
    last = pl.num_programs(1) - 1
    seqs = len_ref.shape[0]
    rows_all = nrm1_ref.shape[0]
    tgt = rows_all // seqs
    half = rows_all // 2
    width = nrm1_ref.shape[1]
    strip = wff_ref.shape[0] // (win_ref.shape[1] // (SPREAD * STRIP))
    wff = stacked(
        [
            wff_ref[c : c + strip, b * width : (b + 1) * width]
            for c in range(0, wff_ref.shape[0], strip)
            for b in range(SPREAD)
        ]
    )

    cot_in = pltpu.make_async_copy(cot_ref, cot_here, sems.at[0])
    down_in = pltpu.make_async_copy(down_ref, down_here, sems.at[1])
    up_in = pltpu.make_async_copy(up_ref, up_here, sems.at[2])
    out_back = pltpu.make_async_copy(out_here, out_ref, sems.at[3])
    adapt_back = pltpu.make_async_copy(adapt_here, adapt_ref, sems.at[4])

    @pl.when((phase == 0) & (j == 0))
    def _():
        down_in.start()
        up_in.start()
        cot_in.start()
        for b in range(2):
            r = pl.ds(b * half, half)
            first = nrm1_ref[r, :] * norm_ref[0:1, :] + norm_ref[1:2, :]
            nrm, inv = norm_stats(first + dot_nn(att_ref[r, :], wco_ref[...]))
            nrm2_ref[r, :] = nrm
            inv2_ref[r, :] = inv
            second = nrm * norm_ref[2:3, :] + norm_ref[3:4, :]
            low_ref[r, :] = second.astype(BF)
            acc_ref[r, :] = second

    @pl.when(phase == 0)
    def _():
        act, slope = gelu_both(dot_nn(low_ref[...], win_ref[...]))
        slope_ref[j] = slope.astype(BF)
        acc_ref[...] += dot_nn(act.astype(BF), wff)

    @pl.when((phase == 1) & (j == 0))
    def _():
        down_in.wait()
        up_in.wait()
        cot_in.wait()
        act, slope = gelu_both(dot_nn(low_ref[...], down_here[...]) + db_ref[...])
        aact_ref[...] = act.astype(BF)
        aslope_ref[...] = slope.astype(BF)
        for s in range(seqs):
            r = pl.ds(s * tgt, tgt)
            adapted = dot_nn(aact_ref[r, :], up_here[...]) + ub_ref[...]
            nrm, inv = norm_stats(acc_ref[r, :] + 4.0 * adapted)
            out_here[r, :] = (nrm * norm_ref[4:5, :] + norm_ref[5:6, :]).astype(BF)
            live = lax.broadcasted_iota(jnp.int32, (tgt, 1), 0) < len_ref[s]
            go = jnp.where(live, cot_here[r, :].astype(F32), 0.0)
            gthree = norm_back(go, nrm, inv, norm_ref[4:5, :])
            g_ref[r, :] = gthree.astype(BF)
            acc_ref[r, :] = gthree
        out_back.start()
        agrad = g_ref[...] * 4.0
        adapt = aact_ref.shape[1]
        apg = (dot_nt(agrad, up_here[...]) * aslope_ref[...].astype(F32)).astype(BF)
        adapt_here[:, :adapt] = dot_tn(low_ref[...], apg).astype(BF)
        adapt_here[:, adapt : 2 * adapt] = dot_tn(agrad, aact_ref[...]).astype(BF)
        ones = jnp.ones((rows_all, PAIR), BF)
        down_sum = dot_tn(apg, ones).astype(BF)
        high = width // adapt
        row = lax.broadcasted_iota(jnp.int32, (width, adapt), 0)
        col = lax.broadcasted_iota(jnp.int32, (width, adapt), 1)
        block = BIAS_ROWS * high
        entry = lax.div(row, block) * BIAS_ROWS + lax.rem(row, block)
        chosen = (entry == col) & (lax.rem(row, block) < BIAS_ROWS)
        placed = dot_nn(jnp.where(chosen, 1.0, 0.0).astype(BF), down_sum)
        lane = lax.broadcasted_iota(jnp.int32, (width, PAIR), 1)
        sums = jnp.where(lane == 2 * PREFIX_PAD, dot_tn(agrad, ones), placed)
        sums = jnp.where((lane >= 2 * PREFIX_PAD) & (lane < 2 * PREFIX_PAD + 2), sums, 0.0)
        adapt_here[:, 2 * adapt :] = sums.astype(BF)
        adapt_back.start()
        acc_ref[...] += dot_nt(apg, down_here[...])

    @pl.when(phase == 1)
    def _():
        grad = (dot_nt(g_ref[...], wff) * slope_ref[j].astype(F32)).astype(BF)
        acc_ref[...] += dot_nt(grad, win_ref[...])

    @pl.when((phase == 1) & (j == last))
    def _():
        gtwo_ref[...] = norm_back(acc_ref[...], nrm2_ref[...], inv2_ref[...], norm_ref[2:3, :])
        out_back.wait()
        adapt_back.wait()


def cross_backward_kernel(
    len_ref, gtwo_ref, wco_ref, cq_ref, mk_ref, mv_ref, wk_ref, wv_ref, late_ref, nrm1_ref,
    inv1_ref, norm_ref,
    dmem_ref, gone_ref, gone_low_ref,
    low_ref, acc_ref, dk_ref, dv_ref, dq_ref, wcq_here, nrm1_here, sems,
):
    step = pl.program_id(0)
    seqs = len_ref.shape[0]
    tgt = cq_ref.shape[0] // seqs
    src = mk_ref.shape[0] // seqs
    width = gtwo_ref.shape[1]
    copies = [
        pltpu.make_async_copy(late_ref.at[:, pl.ds(CQ_AT, width)], wcq_here, sems.at[0]),
        pltpu.make_async_copy(nrm1_ref, nrm1_here, sems.at[1]),
    ]

    @pl.when(step == 0)
    def _():
        for copy in copies:
            copy.start()
        low_ref[...] = gtwo_ref[...].astype(BF)
        acc_ref[...] = jnp.zeros_like(acc_ref)

    mg_all = dot_nt(low_ref[...], wco_ref[...]).astype(BF)
    heads = GROUP // HEAD_DIM
    slot = lax.broadcasted_iota(jnp.int32, (src, tgt), 0)
    for s in range(seqs):
        bias = jnp.where(slot < len_ref[s], 0.0, NEGATIVE)
        here = pl.ds(s * tgt, tgt)
        there = pl.ds(s * src, src)
        q = cq_ref[here, :] * SCALE
        mg = mg_all[s * tgt : (s + 1) * tgt]
        k = mk_ref[there, :]
        scores = cut(dot_nt(stacked(per_head(k)), q), heads, 0)
        dprobs = cut(dot_nt(stacked(per_head(mv_ref[there, :])), mg), heads, 0)
        probs, grads = [], []
        for x, d in zip(scores, dprobs):
            x = x + bias
            x = jnp.exp(x - jnp.max(x, axis=0, keepdims=True))
            x = x * (1.0 / jnp.sum(x, axis=0, keepdims=True))
            grads.append((x * (d - jnp.sum(x * d, axis=0, keepdims=True))).astype(BF))
            probs.append(x.astype(BF))
        dq = dot_tn(stacked(grads), stacked(per_head(k)))
        lanes = pl.ds(pl.multiple_of(step * GROUP, GROUP), GROUP)
        dq_ref[here, lanes] = (dq * SCALE).astype(BF)
        dk_ref[there, :] = dot_nn(beside(grads), stacked(per_head(q))).astype(BF)
        dv_ref[there, :] = dot_nn(beside(probs), stacked(per_head(mg))).astype(BF)
    acc_ref[...] += dot_nt(
        beside([dk_ref[...], dv_ref[...]]), beside([wk_ref[...], wv_ref[...]])
    )

    @pl.when(step == pl.num_programs(0) - 1)
    def _():
        parts, _, high, width = dmem_ref.shape
        for s in range(seqs):
            block = acc_ref[s * src : (s + 1) * src, :]
            dmem_ref[:, s] = block.reshape(parts, high, width).astype(BF)
        for copy in copies:
            copy.wait()
        grad_first = gtwo_ref[...] + dot_nt(dq_ref[...], wcq_here[...])
        grad_one = norm_back(grad_first, nrm1_here[...], inv1_ref[...], norm_ref[0:1, :])
        gone_ref[...] = grad_one
        gone_low_ref[...] = grad_one.astype(BF)


def self_backward_kernel(
    len_ref, low_ref, wo_ref, q_ref, k_ref, v_ref, pk_ref, pv_ref,
    dq_ref, dk_ref, dv_ref, small_ref,
):
    seqs = len_ref.shape[0]
    tgt = low_ref.shape[0] // seqs
    ag_all = dot_nt(low_ref[...], wo_ref[...]).astype(BF)
    heads = GROUP // HEAD_DIM
    row = lax.broadcasted_iota(jnp.int32, (tgt, tgt), 1)
    col = lax.broadcasted_iota(jnp.int32, (tgt, tgt), 0)
    prefix_bias = jnp.where(
        lax.broadcasted_iota(jnp.int32, (PREFIX_PAD, tgt), 0) < PREFIX, 0.0, NEGATIVE
    )
    pk = per_head(pk_ref[...])
    pv = per_head(pv_ref[...])
    dpk = jnp.zeros((PREFIX_PAD, GROUP), F32)
    dpv = jnp.zeros((PREFIX_PAD, GROUP), F32)
    split = heads * PREFIX_PAD
    for s in range(seqs):
        bias = jnp.where((col <= row) & (col < len_ref[s]), 0.0, NEGATIVE)
        here = pl.ds(s * tgt, tgt)
        q = q_ref[here, :] * SCALE
        ag = ag_all[s * tgt : (s + 1) * tgt]
        keys = stacked(pk + per_head(k_ref[here, :]))
        scores = dot_nt(keys, q)
        dprobs = dot_nt(stacked(pv + per_head(v_ref[here, :])), ag)
        probs, grads = [], []
        for x, d, y, e in zip(
            cut(scores[split:], heads, 0),
            cut(dprobs[split:], heads, 0),
            cut(scores[:split], heads, 0),
            cut(dprobs[:split], heads, 0),
        ):
            x = x + bias
            y = y + prefix_bias
            top = jnp.maximum(jnp.max(x, axis=0, keepdims=True), jnp.max(y, axis=0, keepdims=True))
            x = jnp.exp(x - top)
            y = jnp.exp(y - top)
            inv = 1.0 / (jnp.sum(x, axis=0, keepdims=True) + jnp.sum(y, axis=0, keepdims=True))
            x = x * inv
            y = y * inv
            delta = jnp.sum(x * d, axis=0, keepdims=True) + jnp.sum(y * e, axis=0, keepdims=True)
            grads.append([(y * (e - delta)).astype(BF), (x * (d - delta)).astype(BF)])
            probs.append(stacked([y.astype(BF), x.astype(BF)]))
        dq = dot_tn(stacked([g[0] for g in grads] + [g[1] for g in grads]), keys)
        dk = dot_nn(beside([stacked(g) for g in grads]), stacked(per_head(q)))
        dv = dot_nn(beside(probs), stacked(per_head(ag)))
        dq_ref[here, :] = (dq * SCALE).astype(BF)
        dk_ref[here, :] = dk[PREFIX_PAD:].astype(BF)
        dv_ref[here, :] = dv[PREFIX_PAD:].astype(BF)
        dpk = dpk + dk[:PREFIX_PAD]
        dpv = dpv + dv[:PREFIX_PAD]
    for p in range(GROUP // PAIR):
        at = slice(p * PAIR, (p + 1) * PAIR)
        both = stacked(
            [dpk[:, at], dpv[:, at], jnp.zeros((PAIR - 2 * PREFIX_PAD, PAIR), F32)]
        )
        small_ref[at, :] = both.T


def input_grad_kernel(gone_ref, dq_ref, dk_ref, dv_ref, wq_ref, wk_ref, wv_ref, din_ref):
    din_ref[...] = (
        gone_ref[...]
        + dot_nt(
            beside([dq_ref[...], dk_ref[...], dv_ref[...]]),
            beside([wq_ref[...], wk_ref[...], wv_ref[...]]),
        )
    ).astype(BF)


ANYWHERE = pl.BlockSpec(memory_space=pl.ANY)


def square(width, at):
    return pl.BlockSpec((width, width), lambda *_: (0, at // width))


def whole(shape):
    return pl.BlockSpec(shape, lambda *_: (0,) * len(shape))


def columns(rows, width, offset=0):
    return pl.BlockSpec((rows, width), lambda i, *_: (0, i + offset))


def rows_of(height, width, at):
    return pl.BlockSpec((height, width), lambda i, *_: (i, at // width))


def shaped(shape, dtype):
    return jax.ShapeDtypeStruct(shape, dtype)


def call(kernel, grid, in_specs, out_specs, outs, scratch, flops, moved, *args):
    return pl.pallas_call(
        kernel,
        grid_spec=pltpu.PrefetchScalarGridSpec(
            num_scalar_prefetch=1,
            grid=grid,
            in_specs=in_specs,
            out_specs=out_specs,
            scratch_shapes=scratch,
        ),
        out_shape=outs,
        compiler_params=pltpu.CompilerParams(
            vmem_limit_bytes=VMEM_BYTES,
            dimension_semantics=("arbitrary",) * len(grid),
        ),
        cost_estimate=pl.CostEstimate(flops=flops, bytes_accessed=moved, transcendentals=0),
    )(*args)


def self_forward(lens, tok, early, pk, pv):
    rows, width = tok.shape
    steps = width // GROUP
    return call(
        self_forward_kernel,
        (steps,),
        [
            whole((rows, width)),
            columns(width, GROUP),
            columns(width, GROUP, steps),
            columns(width, GROUP, 2 * steps),
            columns(PREFIX_PAD, GROUP),
            columns(PREFIX_PAD, GROUP),
        ],
        [columns(rows, GROUP)] * 4,
        [shaped((rows, width), BF)] * 4,
        [],
        2 * rows * width * width * 3,
        14 * width * width,
        lens, tok, early, early, early, pk, pv,
    )


def cross_forward(lens, mem, late, tok, att, norms):
    rows, width = tok.shape
    steps = width // GROUP
    places = mem.shape[0]
    return call(
        cross_forward_kernel,
        (steps,),
        [
            whole((places, width)),
            columns(width, GROUP, KV_AT // GROUP),
            columns(width, GROUP, KV_AT // GROUP + steps),
            whole((rows, width)),
            whole((rows, width)),
            square(width, SOUT_AT),
            square(width, CQ_AT),
            whole(norms.shape),
        ],
        [columns(places, GROUP)] * 2
        + [whole((rows, width)), whole((rows, width)), whole((rows, 1)), columns(rows, GROUP)],
        [shaped((places, width), BF)] * 2
        + [shaped((rows, width), BF), shaped((rows, width), F32), shaped((rows, 1), F32)]
        + [shaped((rows, width), BF)],
        [],
        2 * width * width * (2 * rows + 2 * places),
        16 * width * width,
        lens, mem, late, late, tok, att, late, late, norms,
    )


def ffn(lens, nrm1, att, cot, late, down, db, up, ub, norms):
    rows, width = nrm1.shape
    hidden = SPREAD * width
    adapt = down.shape[1]
    block = FFN_BLOCK
    steps = hidden // block
    return call(
        ffn_kernel,
        (2, steps),
        [
            whole((rows, width)),
            whole((rows, width)),
            square(width, OUT_AT),
            ANYWHERE,
            pl.BlockSpec((width, block), lambda p, j, *_: (0, j + IN_AT // block)),
            pl.BlockSpec((block // SPREAD, SPREAD * width), lambda p, j, *_: (j, FF_AT)),
            ANYWHERE,
            whole((1, adapt)),
            ANYWHERE,
            whole((1, width)),
            whole(norms.shape),
        ],
        [ANYWHERE, whole((rows, width)), ANYWHERE],
        [
            shaped((rows, width), BF),
            shaped((rows, width), F32),
            shaped((width, 2 * adapt + PAIR), BF),
        ],
        [
            pltpu.VMEM((rows, width), F32),
            pltpu.VMEM((rows, 1), F32),
            pltpu.VMEM((rows, width), F32),
            pltpu.VMEM((rows, width), BF),
            pltpu.VMEM((steps, rows, block), BF),
            pltpu.VMEM((rows, adapt), BF),
            pltpu.VMEM((rows, adapt), BF),
            pltpu.VMEM((rows, width), BF),
            pltpu.VMEM((rows, width), BF),
            pltpu.VMEM((width, adapt), BF),
            pltpu.VMEM((adapt, width), BF),
            pltpu.VMEM((rows, width), BF),
            pltpu.VMEM((width, 2 * adapt + PAIR), BF),
            pltpu.SemaphoreType.DMA((5,)),
        ],
        2 * rows * width * (4 * hidden + 6 * adapt),
        8 * width * hidden,
        lens, nrm1, att, late, cot, late, late, down, db, up, ub, norms,
    )


def cross_backward(lens, gtwo, late, cq, mk, mv, nrm1, inv1, norms, parts):
    rows, width = cq.shape
    steps = width // GROUP
    places = mk.shape[0]
    seqs = lens.shape[0]
    sent = (parts, seqs, places // seqs // parts, width)
    return call(
        cross_backward_kernel,
        (steps,),
        [
            whole((rows, width)),
            rows_of(GROUP, width, OUT_AT),
            columns(rows, GROUP),
            columns(places, GROUP),
            columns(places, GROUP),
            columns(width, GROUP, KV_AT // GROUP),
            columns(width, GROUP, KV_AT // GROUP + steps),
            ANYWHERE,
            ANYWHERE,
            whole((rows, 1)),
            whole(norms.shape),
        ],
        [whole(sent), whole((rows, width)), whole((rows, width))],
        [shaped(sent, BF), shaped((rows, width), F32), shaped((rows, width), BF)],
        [
            pltpu.VMEM((rows, width), BF),
            pltpu.VMEM((places, width), F32),
            pltpu.VMEM((places, GROUP), BF),
            pltpu.VMEM((places, GROUP), BF),
            pltpu.VMEM((rows, width), BF),
            pltpu.VMEM((width, width), BF),
            pltpu.VMEM((rows, width), F32),
            pltpu.SemaphoreType.DMA((2,)),
        ],
        2 * width * width * (rows + 2 * places),
        14 * width * width,
        lens, gtwo, late, cq, mk, mv, late, late, late, nrm1, inv1, norms,
    )


def self_backward(lens, gone_low, late, q, k, v, pk, pv):
    rows, width = q.shape
    steps = width // GROUP
    return call(
        self_backward_kernel,
        (steps,),
        [whole((rows, width)), rows_of(GROUP, width, SOUT_AT)]
        + [columns(rows, GROUP)] * 3
        + [columns(PREFIX_PAD, GROUP)] * 2,
        [columns(rows, GROUP)] * 3 + [pl.BlockSpec((GROUP, PAIR), lambda i, *_: (i, 0))],
        [shaped((rows, width), BF)] * 3 + [shaped((width, PAIR), F32)],
        [],
        2 * rows * width * width * 4,
        20 * width * width,
        lens, gone_low, late, q, k, v, pk, pv,
    )


def input_gradient(gone, dq, dk, dv, early):
    rows, width = gone.shape

    def part(index):
        return pl.BlockSpec((GROUP, width), lambda i: (i, index))

    return pl.pallas_call(
        input_grad_kernel,
        grid=(width // GROUP,),
        in_specs=[pl.BlockSpec((rows, GROUP), lambda i: (0, i))]
        + [whole((rows, width))] * 3
        + [part(0), part(1), part(2)],
        out_specs=pl.BlockSpec((rows, GROUP), lambda i: (0, i)),
        out_shape=shaped((rows, width), BF),
        compiler_params=pltpu.CompilerParams(
            vmem_limit_bytes=VMEM_BYTES, dimension_semantics=("arbitrary",)
        ),
        cost_estimate=pl.CostEstimate(
            flops=6 * rows * width * width, bytes_accessed=12 * width * width, transcendentals=0
        ),
    )(gone, dq, dk, dv, early, early, early)


def around(count, by):
    return [(i, (i + by) % count) for i in range(count)]


def ring_gather(shard, other):
    rows = shard.shape[0]
    half = rows // 2
    count = lax.axis_size("dp_0")
    x, core = lax.axis_index("dp_0"), lax.axis_index("dp_1")
    below = lax.ppermute(shard, "dp_0", around(count, 1))
    above = lax.ppermute(shard, "dp_0", around(count, -1))
    filled = jnp.zeros((count * 2 * rows, shard.shape[1]), shard.dtype)
    filled, other = lax.optimization_barrier((filled, other))
    far_low = lax.ppermute(below[:half], "dp_0", around(count, 1))
    far_high = lax.ppermute(above[half:], "dp_0", around(count, -1))
    for piece, offset, start in (
        (shard, 0, 0), (below, -1, 0), (above, 1, 0), (far_low, 2, 0), (far_high, 2, half),
    ):
        swapped = lax.ppermute(piece, "dp_1", around(2, 1))
        chip = (x + offset + count) % count
        for part, place in ((piece, core), (swapped, 1 - core)):
            at = (chip * 2 + place) * rows + start
            filled = lax.dynamic_update_slice_in_dim(filled, part, at, 0)
    return filled, other


def scatter_sum(blocks):
    count = lax.axis_size("dp_0")
    x, core = lax.axis_index("dp_0"), lax.axis_index("dp_1")
    by_core = blocks.reshape(count, 2, *blocks.shape[1:])
    kept = lax.dynamic_index_in_dim(by_core, core, 1, keepdims=False)
    given = lax.dynamic_index_in_dim(by_core, 1 - core, 1, keepdims=False)
    paired = kept + lax.ppermute(given, "dp_1", around(2, 1))
    total = lax.dynamic_index_in_dim(paired, x, 0, keepdims=False)
    for by in range(1, count):
        sent = lax.dynamic_index_in_dim(paired, (x + by) % count, 0, keepdims=False)
        total = total + lax.ppermute(sent, "dp_0", around(count, by))
    return total


def local(
    tokens, memory, cotangent, tgt_len, src_len,
    self_qkv, self_out, cross_q, cross_kv, cross_out, ffn_in, ffn_out,
    first_gain, first_bias, second_gain, second_bias, third_gain, third_bias,
    prefix_key, prefix_value, down_weight, down_bias, up_weight, up_bias,
):
    mem_groups = lax.axis_size(MEM)
    mem_place = lax.axis_index(MEM)
    seqs, tgt, width = tokens.shape
    src_block = memory.shape[1]
    prefix = prefix_key.shape[0]

    high = cross_out.shape[0] // mem_groups
    mine = functools.partial(
        lax.dynamic_slice_in_dim, start_index=mem_place * high, slice_size=high
    )
    spread = mine(ffn_out.reshape(SPREAD, -1, width), axis=1)
    late = lax.all_gather(
        jnp.concatenate(
            [jnp.moveaxis(spread, 0, 1).reshape(high, SPREAD * width)]
            + [mine(w, axis=0) for w in (ffn_in, cross_out, self_out, cross_q, cross_kv)],
            axis=1,
        ),
        DP_MEM, axis=0, tiled=True,
    )
    early, memory = ring_gather(self_qkv, memory)
    mem_rows = lax.all_to_all(memory, MEM, split_axis=0, concat_axis=1, tiled=True)
    mem_rows = mem_rows.reshape(-1, width)
    own_src = lax.dynamic_slice_in_dim(src_len, mem_place * seqs, seqs, 0)

    tok = tokens.reshape(seqs * tgt, width)
    cot = cotangent.reshape(seqs * tgt, width)
    pk = jnp.pad(prefix_key, ((0, PREFIX_PAD - prefix), (0, 0)))
    pv = jnp.pad(prefix_value, ((0, PREFIX_PAD - prefix), (0, 0)))

    q, k, v, att = self_forward(tgt_len, tok, early, pk, pv)
    vectors = jnp.stack(
        [first_gain, first_bias, second_gain, second_bias, third_gain, third_bias]
        + [third_bias] * 2
    )
    vectors, att = lax.optimization_barrier((vectors, att))
    norms = lax.all_gather(vectors, DP, axis=1, tiled=True).astype(F32)
    mk, mv, cq, nrm1, inv1, cross = cross_forward(own_src, mem_rows, late, tok, att, norms)
    output, gtwo, adapter = ffn(
        tgt_len, nrm1, cross, cot, late,
        down_weight, down_bias.astype(F32)[None], up_weight, up_bias.astype(F32)[None], norms,
    )
    adapter = lax.psum_scatter(adapter, DP, scatter_dimension=0, tiled=True)

    dmem, gone, gone_low = cross_backward(
        own_src, gtwo, late, cq, mk, mv, nrm1, inv1, norms, mem_groups
    )
    memory_grad = lax.all_to_all(dmem, MEM, split_axis=0, concat_axis=0, tiled=True)
    dq, dk, dv, small = self_backward(tgt_len, gone_low, late, q, k, v, pk, pv)
    small = scatter_sum(small.reshape(lax.axis_size(DP), -1, PAIR))
    dq, small, memory_grad = lax.optimization_barrier((dq, small, memory_grad))
    din = input_gradient(gone, dq, dk, dv, early)
    adapt = down_weight.shape[1]
    joined = (adapter.astype(F32) + jnp.pad(small, ((0, 0), (2 * adapt, 0)))).astype(BF)
    arrived = lax.all_to_all(
        joined.reshape(mem_groups, -1, joined.shape[1]),
        MEM, split_axis=0, concat_axis=0, tiled=True,
    )
    down_grad, up_grad, last = (
        jnp.sum(arrived[..., a:b].astype(F32), axis=0)
        for a, b in ((0, adapt), (adapt, 2 * adapt), (2 * adapt, joined.shape[1]))
    )
    return (
        output.reshape(tokens.shape),
        din.reshape(tokens.shape),
        memory_grad.reshape(memory.shape),
        last[:, :prefix].T,
        last[:, PREFIX_PAD : PREFIX_PAD + prefix].T,
        down_grad,
        last[:BIAS_ROWS, 2 * PREFIX_PAD + 1],
        up_grad.T,
        last[:, 2 * PREFIX_PAD],
    )


def solution(mesh):
    torus = Mesh(mesh.devices.reshape(4, 2, 4, 4), ("dp_0", "dp_1", "mem_0", "mem_1"))
    by_dp = P(DP, None)
    copied = P(None)
    return jax.shard_map(
        local,
        mesh=torus,
        in_specs=(
            P(DP_MEM, None, None), P(DP, MEM, None), P(DP_MEM, None, None), P(DP_MEM), P(DP),
            by_dp, by_dp, by_dp, by_dp, by_dp, by_dp, by_dp,
            P(DP), P(DP), P(DP), P(DP), P(DP), P(DP),
            copied, copied, copied, copied, copied, copied,
        ),
        out_specs=(
            P(DP_MEM, None, None),
            P(DP_MEM, None, None),
            P(DP, MEM, None),
            P(None, DP_MEM),
            P(None, DP_MEM),
            P(DP_MEM, None),
            P(DP_MEM),
            P(None, DP_MEM),
            P(DP_MEM),
        ),
        check_vma=False,
    )
```

profile of v0, /device:TPU:0, one launch (start us, length us, event | category | flops | bytes accessed | tf_op | source)
XLA Modules:
  0.0 266.9 jit_solution(13471220565480420507)
XLA Ops:
  7.3 0.0 all-gather.2.cloned.1.call-start
  7.3 1.1 copy-done
  8.5 0.9 dynamic-slice_dynamic-update-slice_fusion
  9.3 0.7 dynamic-slice_dynamic-update-slice_fusion.4
  10.1 0.7 dynamic-slice_dynamic-update-slice_fusion.3
  10.8 0.7 dynamic-slice_dynamic-update-slice_fusion.2
  11.5 0.8 dynamic-slice_dynamic-update-slice_fusion.1
  12.3 0.7 copy-done.3
  13.0 1.6 collective-permute-start.1
  14.6 1.7 collective-permute-start.3
  16.3 8.1 %all-to-all-start = ((bf16[32,24,1024]{2,1,0:T(8,128)(2,1)}), bf16[32,24,1024]{2,1,0:T(8,128)(2,1)S(1)}, u32[]{:S(2)}, u32[]{:S(2)}) async-start(bf16[32,24,1024]{2,1,0:T(8,128)(2,1)} %param.25), calls=%async_computation | async-start | bytes 3145728 | tf_op jit(solution)/shard_map/all_to_all | solution.py:708
  24.4 0.0 reduce-scatter.2.cloned.1.call-start
  24.5 10.1 %collective-permute-done.1 = bf16[128,3072]{1,0:T(8,128)(2,1)S(1)} collective-permute-done((bf16[128,3072]{1,0:T(8,128)(2,1)}, bf16[128,3072]{1,0:T(8,128)(2,1)S(1)}, u32[]{:S(2)}, u32[]{:S(2)}) %collective-permute-start.1) | collective-permute-done | bytes 786464 | tf_op jit(solution)/shard_map/ppermute | solution.py:651
  34.6 3.4 %broadcast_in_dim.13 = bf16[1024,3072]{1,0:T(8,128)(2,1)} broadcast(bf16[]{:T(256)} %constant.88.clone.1), dimensions={} | broadcast | bytes 6291458 | tf_op jit(solution)/shard_map/broadcast_in_dim | solution.py:653
  38.0 1.0 constant_dynamic-update-slice_fusion.10
  39.0 0.6 pad.11.pk_ref
  39.6 0.6 pad.12.pv_ref
  40.2 0.6 broadcast_in_dim.19
  40.8 0.6 broadcast_in_dim.18
  41.4 0.6 dynamic_slice.41.len_ref
  42.1 0.7 collective-permute-start.5
  42.8 2.7 %collective-permute-start.7 = (bf16[64,3072]{1,0:T(8,128)(2,1)S(1)}, bf16[64,3072]{1,0:T(8,128)(2,1)}, u32[]{:S(2)}, u32[]{:S(2)}) collective-permute-start(bf16[64,3072]{1,0:T(8,128)(2,1)S(1)} %slice.37), channel_id=1, source_target_pairs={{0,96},{32,0},{64,32},{96,64},{1,97},{33,1},{65,33},{97,65},{2,98}... | collective-permute-start | bytes 1179656 | tf_op jit(solution)/shard_map/ppermute | solution.py:656
  45.5 2.1 constant_dynamic-update-slice_fusion.9
  47.6 1.0 constant_dynamic-update-slice_fusion.8
  48.5 6.8 %collective-permute-done.5 = bf16[64,3072]{1,0:T(8,128)(2,1)} collective-permute-done((bf16[64,3072]{1,0:T(8,128)(2,1)S(1)}, bf16[64,3072]{1,0:T(8,128)(2,1)}, u32[]{:S(2)}, u32[]{:S(2)}) %collective-permute-start.5) | collective-permute-done | bytes 393248 | tf_op jit(solution)/shard_map/ppermute | solution.py:655
  55.4 0.5 collective-permute-start.8
  55.9 1.3 copy.34
  57.2 2.1 constant_dynamic-update-slice_fusion.7
  59.3 1.0 constant_dynamic-update-slice_fusion.6
  60.2 2.1 constant_dynamic-update-slice_fusion.5
  62.3 1.8 constant_dynamic-update-slice_fusion.4
  64.1 1.8 constant_dynamic-update-slice_fusion.3
  65.9 1.8 constant_dynamic-update-slice_fusion.2
  67.7 1.8 constant_dynamic-update-slice_fusion.1.wq_ref.wk_ref.wv_ref
  69.5 12.7 %shard_map.295 = (bf16[512,1024]{1,0:T(8,128)(2,1)}, bf16[512,1024]{1,0:T(8,128)(2,1)}, bf16[512,1024]{1,0:T(8,128)(2,1)}, bf16[512,1024]{1,0:T(8,128)(2,1)}) custom-call(s32[2]{0:T(128)} %len_ref.5, bf16[512,1024]{1,0:T(8,128)(2,1)} %bitcast.49, bf16[1024,3072]{1,0:T(8,128)(2,1)} %constant_dynamic-update-slice_fusion.1.wq_ref.wk_ref.wv_ref, ...), custom_call_target="tpu_custom_call" | custom-call | flops 3221225472 | bytes 14680064 | tf_op jit(solution)/shard_map/pallas_call | solution.py:441
  82.2 11.2 %all_gather.7 = bf16[8,1024]{1,0:T(8,128)(2,1)S(1)} all-gather(bf16[8,128]{1,0:T(8,128)(2,1)S(1)} %stack.29), channel_id=1, replica_groups=mesh['dp_0'=4,'dp_1'=2,'mem_0'=4,'mem_1'=4] {'dp_0','dp_1'}, dimensions={1}, use_global_device_ids=true | all-gather | bytes 18432 | tf_op jit(solution)/shard_map/all_gather | solution.py:723
  93.4 0.6 convert_element_type.25.norm_ref
  94.0 29.2 %all-gather.2.cloned.1.call-done.wk_ref.wv_ref.wo_ref.wcq_ref.wco_ref.win_ref.wff_ref.late_ref = bf16[1024,13312]{1,0:T(8,128)(2,1)} async-done(((bf16[8,13312]{1,0:T(8,128)(2,1)}), bf16[1024,13312]{1,0:T(8,128)(2,1)}) %all-gather.2.cloned.1.call-update) | async-done | bytes 27262992 | tf_op jit(solution)/shard_map/all_gather | solution.py:699
  123.2 18.7 %shard_map.296 = (bf16[768,1024]{1,0:T(8,128)(2,1)}, bf16[768,1024]{1,0:T(8,128)(2,1)}, bf16[512,1024]{1,0:T(8,128)(2,1)}, f32[512,1024]{1,0:T(8,128)}, f32[512,1]{1,0:T(8,128)}, /*index=5*/bf16[512,1024]{1,0:T(8,128)(2,1)}) custom-call(s32[2]{0:T(128)} %dynamic_slice.41.len_ref, bf16[768,1024]{1,0:T(8,128)(2,1)} %bitcast.48, ...), custom_call_target="tpu_custom_call" | custom-call | flops 5368709120 | bytes 16777216 | tf_op jit(solution)/shard_map/pallas_call | solution.py:441
  141.9 35.9 %shard_map.297 = (bf16[512,1024]{1,0:T(8,128)(2,1)}, f32[512,1024]{1,0:T(8,128)}, bf16[1024,1152]{1,0:T(8,128)(2,1)}) custom-call(s32[2]{0:T(128)} %len_ref.5, f32[512,1024]{1,0:T(8,128)} %get-tuple-element.41.nrm1_ref, bf16[512,1024]{1,0:T(8,128)(2,1)} %get-tuple-element.42.att_ref, ...), custom_call_target="tpu_custom_call" | custom-call | flops 20401094656 | bytes 33554432 | tf_op jit(solution)/shard_map/pallas_call | solution.py:441
  177.8 0.0 reduce-scatter.2.cloned.1.call-update
  177.8 26.0 %shard_map.298 = (bf16[16,2,24,1024]{3,2,1,0:T(8,128)(2,1)}, f32[512,1024]{1,0:T(8,128)}, bf16[512,1024]{1,0:T(8,128)(2,1)}) custom-call(s32[2]{0:T(128)} %dynamic_slice.41.len_ref, f32[512,1024]{1,0:T(8,128)} %get-tuple-element.44.gtwo_ref, bf16[1024,13312]{1,0:T(8,128)(2,1)} %all-gather.2.cloned.1.call-done.wk_ref.wv_ref.wo_ref.wcq_ref.wco_ref.win_ref.wff_ref.late_ref, ...), custom_call_target="tpu_custom_call" | custom-call | flops 4294967296 | bytes 14680064 | tf_op jit(solution)/shard_map/pallas_call | solution.py:441
  203.8 6.0 %all-to-all-start.1 = ((bf16[16,2,24,1024]{3,2,1,0:T(8,128)(2,1)}), bf16[16,2,24,1024]{3,2,1,0:T(8,128)(2,1)S(1)}, u32[]{:S(2)}, u32[]{:S(2)}) async-start(bf16[16,2,24,1024]{3,2,1,0:T(8,128)(2,1)} %get-tuple-element.56), calls=%async_computation.1 | async-start | bytes 3145728 | tf_op jit(solution)/shard_map/all_to_all | solution.py:734
  209.8 17.4 %shard_map.299 = (bf16[512,1024]{1,0:T(8,128)(2,1)}, bf16[512,1024]{1,0:T(8,128)(2,1)}, bf16[512,1024]{1,0:T(8,128)(2,1)}, f32[1024,128]{1,0:T(8,128)}) custom-call(s32[2]{0:T(128)} %len_ref.5, bf16[512,1024]{1,0:T(8,128)(2,1)} %get-tuple-element.50.low_ref, ...), custom_call_target="tpu_custom_call" | custom-call | flops 4294967296 | bytes 20971520 | tf_op jit(solution)/shard_map/pallas_call | solution.py:441
  227.2 1.0 dynamic-slice_bitcast_fusion
  228.1 0.1 collective-permute-start.9
  228.3 1.5 collective-permute-done.9
  229.7 1.0 bitcast_add_fusion
  230.8 0.6 collective-permute-start.10
  231.4 2.7 %collective-permute-start.11 = (f32[128,128]{1,0:T(8,128)S(1)}, f32[128,128]{1,0:T(8,128)S(1)}, u32[]{:S(2)}, u32[]{:S(2)}) collective-permute-start(f32[128,128]{1,0:T(8,128)S(1)} %get-tuple-element.67), channel_id=1, source_target_pairs={{0,64},{32,96},{64,0},{96,32},{1,65},{33,97},{65,1},{97,33},{2,66}... | collective-permute-start | bytes 196616 | tf_op jit(solution)/shard_map/ppermute | solution.py:678
  234.1 1.5 collective-permute-start.12
  235.5 1.4 collective-permute-done.10
  236.9 0.7 collective-permute-done.11
  237.6 0.8 collective-permute-done.12
  238.4 0.0 reduce-scatter.2.cloned.1.call-done
  238.4 1.7 fusion
  240.1 7.2 %all-to-all-start.2 = ((bf16[16,8,1152]{2,1,0:T(8,128)(2,1)}), bf16[16,8,1152]{2,1,0:T(8,128)(2,1)S(1)}, u32[]{:S(2)}, u32[]{:S(2)}) async-start(bf16[16,8,1152]{2,1,0:T(8,128)(2,1)} %fusion), calls=%async_computation.3 | async-start | bytes 589824 | tf_op jit(solution)/shard_map/all_to_all | solution.py:741
  247.4 8.3 %shard_map.300 = bf16[512,1024]{1,0:T(8,128)(2,1)} custom-call(f32[512,1024]{1,0:T(8,128)} %get-tuple-element.49.gone_ref, bf16[512,1024]{1,0:T(8,128)(2,1)} %get-tuple-element.57.dq_ref, bf16[512,1024]{1,0:T(8,128)(2,1)} %get-tuple-element.58.dk_ref, bf16[512,1024]{1,0:T(8,128)(2,1)} %get-tuple-element.59.dv_ref, ...), custom_call_target="tpu_custom_call" | custom-call | flops 3221225472 | bytes 12582912 | tf_op jit(solution)/shard_map/pallas_call | solution.py:625
  255.7 0.5 all-to-all-done.2
  256.2 0.7 slice_bitcast_fusion
  256.9 0.7 slice_reduce_fusion
  257.6 0.7 slice_reduce_fusion.1
  258.3 0.6 convert_reduce_fusion
  258.9 1.1 copy.51
  (50 shorter events, 0.3 us)
Async XLA Ops:
  7.2 1.2 copy-start
  7.2 31.8 %copy-start.4 = (bf16[30,1024]{1,0:T(8,128)(2,1)S(1)}, bf16[30,1024]{1,0:T(8,128)(2,1)}, u32[]{:S(2)}) copy-start(bf16[30,1024]{1,0:T(8,128)(2,1)} %param.42) | copy-start | bytes 184324
  7.2 32.4 %copy-start.5 = (bf16[30,1024]{1,0:T(8,128)(2,1)S(1)}, bf16[30,1024]{1,0:T(8,128)(2,1)}, u32[]{:S(2)}) copy-start(bf16[30,1024]{1,0:T(8,128)(2,1)} %param.43) | copy-start | bytes 184324
  7.2 33.0 %copy-start.7 = (bf16[1024]{0:T(1024)(128)(2,1)S(1)}, bf16[1024]{0:T(1024)(128)(2,1)}, u32[]{:S(2)}) copy-start(bf16[1024]{0:T(1024)(128)(2,1)} %param.47) | copy-start | bytes 6148
  7.2 33.6 %copy-start.8 = (bf16[512]{0:T(512)(128)(2,1)S(1)}, bf16[512]{0:T(512)(128)(2,1)}, u32[]{:S(2)}) copy-start(bf16[512]{0:T(512)(128)(2,1)} %param.45) | copy-start | bytes 3076
  7.2 34.7 %copy-start.6 = (bf16[128]{0:T(256)(128)(2,1)S(1)}, bf16[128]{0:T(256)(128)(2,1)}, u32[]{:S(2)}) copy-start(bf16[128]{0:T(256)(128)(2,1)} %param.41) | copy-start | bytes 772
  7.2 34.7 %copy-start.9 = (bf16[128]{0:T(256)(128)(2,1)S(1)}, bf16[128]{0:T(256)(128)(2,1)}, u32[]{:S(2)}) copy-start(bf16[128]{0:T(256)(128)(2,1)} %param.36) | copy-start | bytes 772
  7.3 116.0 %all-gather.2.cloned.1.call-start = ((), (), s32[]{:S(2)}) async-start(), calls=%async_computation.4 | async-start | bytes 27475968 | tf_op jit(solution)/shard_map/all_gather | solution.py:699
  8.4 33.0 %copy-start.14 = (s32[32]{0:T(128)S(1)}, s32[32]{0:T(128)}, u32[]{:S(2)}) copy-start(s32[32]{0:T(128)} %param.28) | copy-start | bytes 388
  8.4 33.6 %copy-start.10 = (bf16[128]{0:T(256)(128)(2,1)S(1)}, bf16[128]{0:T(256)(128)(2,1)}, u32[]{:S(2)}) copy-start(bf16[128]{0:T(256)(128)(2,1)} %param.37) | copy-start | bytes 772
  8.4 33.6 %copy-start.11 = (bf16[128]{0:T(256)(128)(2,1)S(1)}, bf16[128]{0:T(256)(128)(2,1)}, u32[]{:S(2)}) copy-start(bf16[128]{0:T(256)(128)(2,1)} %param.38) | copy-start | bytes 772
  8.4 33.6 %copy-start.12 = (bf16[128]{0:T(256)(128)(2,1)S(1)}, bf16[128]{0:T(256)(128)(2,1)}, u32[]{:S(2)}) copy-start(bf16[128]{0:T(256)(128)(2,1)} %param.39) | copy-start | bytes 772
  8.5 33.6 %copy-start.13 = (bf16[128]{0:T(256)(128)(2,1)S(1)}, bf16[128]{0:T(256)(128)(2,1)}, u32[]{:S(2)}) copy-start(bf16[128]{0:T(256)(128)(2,1)} %param.40) | copy-start | bytes 772
  12.3 0.7 copy-start.3
  13.0 21.6 %collective-permute-start.1 = (bf16[128,3072]{1,0:T(8,128)(2,1)}, bf16[128,3072]{1,0:T(8,128)(2,1)S(1)}, u32[]{:S(2)}, u32[]{:S(2)}) collective-permute-start(bf16[128,3072]{1,0:T(8,128)(2,1)} %param.29), channel_id=1, source_target_pairs={{0,32},{32,64},{64,96},{96,0},{1,33},{33,65},{65,97},{97,1},{2,34}... | collective-permute-start | bytes 2359304 | tf_op jit(solution)/shard_map/ppermute | solution.py:651
  14.6 28.1 %collective-permute-start.3 = (bf16[128,3072]{1,0:T(8,128)(2,1)}, bf16[128,3072]{1,0:T(8,128)(2,1)S(1)}, u32[]{:S(2)}, u32[]{:S(2)}) collective-permute-start(bf16[128,3072]{1,0:T(8,128)(2,1)} %param.29), channel_id=1, source_target_pairs={{0,96},{32,0},{64,32},{96,64},{1,97},{33,1},{65,33},{97,65},{2,98}... | collective-permute-start | bytes 2359304 | tf_op jit(solution)/shard_map/ppermute | solution.py:652
  16.3 29.2 %collective-permute-start = (bf16[128,3072]{1,0:T(8,128)(2,1)}, bf16[128,3072]{1,0:T(8,128)(2,1)}, u32[]{:S(2)}, u32[]{:S(2)}) collective-permute-start(bf16[128,3072]{1,0:T(8,128)(2,1)} %param.29), channel_id=1, source_target_pairs={{0,16},{16,0},{1,17},{17,1},{2,18},{18,2},{3,19},{19,3},{4,20},{20... | collective-permute-start | bytes 2359304 | tf_op jit(solution)/shard_map/ppermute | solution.py:660
  16.3 39.6 %all-to-all-start = ((bf16[32,24,1024]{2,1,0:T(8,128)(2,1)}), bf16[32,24,1024]{2,1,0:T(8,128)(2,1)S(1)}, u32[]{:S(2)}, u32[]{:S(2)}) async-start(bf16[32,24,1024]{2,1,0:T(8,128)(2,1)} %param.25), calls=%async_computation | async-start | bytes 3145728 | tf_op jit(solution)/shard_map/all_to_all | solution.py:708
  24.4 214.0 %reduce-scatter.2.cloned.1.call-start = ((), (), s32[]{:S(2)}) async-start(), calls=%async_computation.5 | async-start | bytes 2654208 | tf_op jit(solution)/shard_map/reduce_scatter | solution.py:729
  24.5 13.5 %copy-start.2 = (bf16[128,3072]{1,0:T(8,128)(2,1)S(1)}, bf16[128,3072]{1,0:T(8,128)(2,1)}, u32[]{:S(2)}) copy-start(bf16[128,3072]{1,0:T(8,128)(2,1)} %param.29) | copy-start | bytes 2359300
  34.6 22.6 %collective-permute-start.2 = (bf16[128,3072]{1,0:T(8,128)(2,1)S(1)}, bf16[128,3072]{1,0:T(8,128)(2,1)}, u32[]{:S(2)}, u32[]{:S(2)}) collective-permute-start(bf16[128,3072]{1,0:T(8,128)(2,1)S(1)} %collective-permute-done.1), channel_id=1, source_target_pairs={{0,16},{16,0},{1,17},{17,1},{2,18},{18,2},{3,19},{19,3},{4,20},{20... | collective-permute-start | bytes 2359304 | tf_op jit(solution)/shard_map/ppermute | solution.py:660
  42.1 13.3 %collective-permute-start.5 = (bf16[64,3072]{1,0:T(8,128)(2,1)S(1)}, bf16[64,3072]{1,0:T(8,128)(2,1)}, u32[]{:S(2)}, u32[]{:S(2)}) collective-permute-start(bf16[64,3072]{1,0:T(8,128)(2,1)S(1)} %slice.36), channel_id=1, source_target_pairs={{0,32},{32,64},{64,96},{96,0},{1,33},{33,65},{65,97},{97,1},{2,34}... | collective-permute-start | bytes 1179656 | tf_op jit(solution)/shard_map/ppermute | solution.py:655
  42.8 12.6 %collective-permute-start.7 = (bf16[64,3072]{1,0:T(8,128)(2,1)S(1)}, bf16[64,3072]{1,0:T(8,128)(2,1)}, u32[]{:S(2)}, u32[]{:S(2)}) collective-permute-start(bf16[64,3072]{1,0:T(8,128)(2,1)S(1)} %slice.37), channel_id=1, source_target_pairs={{0,96},{32,0},{64,32},{96,64},{1,97},{33,1},{65,33},{97,65},{2,98}... | collective-permute-start | bytes 1179656 | tf_op jit(solution)/shard_map/ppermute | solution.py:656
  45.5 14.8 %collective-permute-start.4 = (bf16[128,3072]{1,0:T(8,128)(2,1)S(1)}, bf16[128,3072]{1,0:T(8,128)(2,1)}, u32[]{:S(2)}, u32[]{:S(2)}) collective-permute-start(bf16[128,3072]{1,0:T(8,128)(2,1)S(1)} %collective-permute-done.3), channel_id=1, source_target_pairs={{0,16},{16,0},{1,17},{17,1},{2,18},{18,2},{3,19},{19,3},{4,20},{20... | collective-permute-start | bytes 2359304 | tf_op jit(solution)/shard_map/ppermute | solution.py:660
  55.4 8.8 %collective-permute-start.6 = (bf16[64,3072]{1,0:T(8,128)(2,1)}, bf16[64,3072]{1,0:T(8,128)(2,1)}, u32[]{:S(2)}, u32[]{:S(2)}) collective-permute-start(bf16[64,3072]{1,0:T(8,128)(2,1)} %collective-permute-done.5), channel_id=1, source_target_pairs={{0,16},{16,0},{1,17},{17,1},{2,18},{18,2},{3,19},{19,3},{4,20},{20... | collective-permute-start | bytes 1179656 | tf_op jit(solution)/shard_map/ppermute | solution.py:660
  55.4 12.3 %collective-permute-start.8 = (bf16[64,3072]{1,0:T(8,128)(2,1)}, bf16[64,3072]{1,0:T(8,128)(2,1)}, u32[]{:S(2)}, u32[]{:S(2)}) collective-permute-start(bf16[64,3072]{1,0:T(8,128)(2,1)} %collective-permute-done.7), channel_id=1, source_target_pairs={{0,16},{16,0},{1,17},{17,1},{2,18},{18,2},{3,19},{19,3},{4,20},{20... | collective-permute-start | bytes 1179656 | tf_op jit(solution)/shard_map/ppermute | solution.py:660
  203.8 34.6 %all-to-all-start.1 = ((bf16[16,2,24,1024]{3,2,1,0:T(8,128)(2,1)}), bf16[16,2,24,1024]{3,2,1,0:T(8,128)(2,1)S(1)}, u32[]{:S(2)}, u32[]{:S(2)}) async-start(bf16[16,2,24,1024]{3,2,1,0:T(8,128)(2,1)} %get-tuple-element.56), calls=%async_computation.1 | async-start | bytes 3145728 | tf_op jit(solution)/shard_map/all_to_all | solution.py:734
  228.1 1.6 collective-permute-start.9
  230.8 6.1 %collective-permute-start.10 = (f32[128,128]{1,0:T(8,128)S(1)}, f32[128,128]{1,0:T(8,128)S(1)}, u32[]{:S(2)}, u32[]{:S(2)}) collective-permute-start(f32[128,128]{1,0:T(8,128)S(1)} %get-tuple-element.65), channel_id=1, source_target_pairs={{0,32},{32,64},{64,96},{96,0},{1,33},{33,65},{65,97},{97,1},{2,34}... | collective-permute-start | bytes 196616 | tf_op jit(solution)/shard_map/ppermute | solution.py:678
  231.4 6.2 %collective-permute-start.11 = (f32[128,128]{1,0:T(8,128)S(1)}, f32[128,128]{1,0:T(8,128)S(1)}, u32[]{:S(2)}, u32[]{:S(2)}) collective-permute-start(f32[128,128]{1,0:T(8,128)S(1)} %get-tuple-element.67), channel_id=1, source_target_pairs={{0,64},{32,96},{64,0},{96,32},{1,65},{33,97},{65,1},{97,33},{2,66}... | collective-permute-start | bytes 196616 | tf_op jit(solution)/shard_map/ppermute | solution.py:678
  234.1 4.3 %collective-permute-start.12 = (f32[128,128]{1,0:T(8,128)S(1)}, f32[128,128]{1,0:T(8,128)S(1)}, u32[]{:S(2)}, u32[]{:S(2)}) collective-permute-start(f32[128,128]{1,0:T(8,128)S(1)} %get-tuple-element.66), channel_id=1, source_target_pairs={{0,96},{32,0},{64,32},{96,64},{1,97},{33,1},{65,33},{97,65},{2,98}... | collective-permute-start | bytes 196616 | tf_op jit(solution)/shard_map/ppermute | solution.py:678
  240.1 16.1 %all-to-all-start.2 = ((bf16[16,8,1152]{2,1,0:T(8,128)(2,1)}), bf16[16,8,1152]{2,1,0:T(8,128)(2,1)S(1)}, u32[]{:S(2)}, u32[]{:S(2)}) async-start(bf16[16,8,1152]{2,1,0:T(8,128)(2,1)} %fusion), calls=%async_computation.3 | async-start | bytes 589824 | tf_op jit(solution)/shard_map/all_to_all | solution.py:741
  247.3 12.7 %copy-start.1 = (bf16[512,1024]{1,0:T(8,128)(2,1)S(1)}, bf16[512,1024]{1,0:T(8,128)(2,1)}, u32[]{:S(2)}) copy-start(bf16[512,1024]{1,0:T(8,128)(2,1)} %param.35) | copy-start | bytes 3145732
Sparse Core Ops, SparseCore 0:
  13.1 110.0 all-gather.1
  177.9 33.4 reduce-scatter.1
where the time goes:
time: 268 us; the launch traced here: 267 us
  Pallas kernels  119 us (44%)
  waiting for transfers between devices  51 us (19%)
  starting transfers between devices  33.4 us (12%)
  local copies, waits for them, and re-layouts  32.7 us (12%)
  between operations  14.4 us (5%)
  blocking collectives  11.2 us (4%)
  other arithmetic  5.15 us (2%)
    pallas_call x5, Pallas kernels, call(): pl.pallas_call(kernel, grid_spec=pltpu.PrefetchScalarGridSpec(num_scalar_...  111 us
    all_gather x1, waiting for transfers between devices, local(): lax.all_gather(jnp.concatenate([jnp.moveaxis(spread, 0, 1).reshape(high,...  29.2 us
    dynamic_update_slice x10, local copies, waits for them, and re-layouts, ring_gather(): filled = lax.dynamic_update_slice_in_dim(filled, part, at, 0)  16.3 us
    all_gather x1, blocking collectives, local(): norms = lax.all_gather(vectors, DP, axis=1, tiled=True).astype(F32)  11.2 us
    ppermute x1, waiting for transfers between devices, ring_gather(): below = lax.ppermute(shard, 'dp_0', around(count, 1))  10.1 us
    pallas_call x1, Pallas kernels, input_gradient(): pl.pallas_call(input_grad_kernel, grid=(width // GROUP,), in_specs=[pl.Bl...  8.32 us
    all_to_all x1, starting transfers between devices, local(): lax.all_to_all(memory, MEM, split_axis=0, concat_axis=1, tiled=True)  8.13 us
    all_to_all x1, starting transfers between devices, local(): lax.all_to_all(joined.reshape(mem_groups, -1, joined.shape[1]), MEM, spli...  7.21 us
  transfers between devices with their start and end apart: 18, of which 8 were waited for; matrix products, arithmetic and copies ran while one was open for 10% of the time, Pallas kernels for 24%

commit v1 on v0

--- a/solution.py
+++ b/solution.py
@@ -305,27 +305,35 @@
     mg_all = dot_nt(low_ref[...], wco_ref[...]).astype(BF)
     heads = GROUP // HEAD_DIM
     slot = lax.broadcasted_iota(jnp.int32, (src, tgt), 0)
+    raw = []
+    for s in range(seqs):
+        q = cq_ref[s * tgt : (s + 1) * tgt, :] * SCALE
+        mg = mg_all[s * tgt : (s + 1) * tgt]
+        there = pl.ds(s * src, src)
+        raw.append(
+            (
+                dot_nt(stacked(per_head(mk_ref[there, :])), q),
+                dot_nt(stacked(per_head(mv_ref[there, :])), mg),
+            )
+        )
     for s in range(seqs):
         bias = jnp.where(slot < len_ref[s], 0.0, NEGATIVE)
         here = pl.ds(s * tgt, tgt)
         there = pl.ds(s * src, src)
-        q = cq_ref[here, :] * SCALE
-        mg = mg_all[s * tgt : (s + 1) * tgt]
-        k = mk_ref[there, :]
-        scores = cut(dot_nt(stacked(per_head(k)), q), heads, 0)
-        dprobs = cut(dot_nt(stacked(per_head(mv_ref[there, :])), mg), heads, 0)
         probs, grads = [], []
-        for x, d in zip(scores, dprobs):
+        for x, d in zip(cut(raw[s][0], heads, 0), cut(raw[s][1], heads, 0)):
             x = x + bias
             x = jnp.exp(x - jnp.max(x, axis=0, keepdims=True))
             x = x * (1.0 / jnp.sum(x, axis=0, keepdims=True))
             grads.append((x * (d - jnp.sum(x * d, axis=0, keepdims=True))).astype(BF))
             probs.append(x.astype(BF))
-        dq = dot_tn(stacked(grads), stacked(per_head(k)))
+        q = cq_ref[here, :] * SCALE
+        mg = mg_all[s * tgt : (s + 1) * tgt]
+        dv_ref[there, :] = dot_nn(beside(probs), stacked(per_head(mg))).astype(BF)
+        dk_ref[there, :] = dot_nn(beside(grads), stacked(per_head(q))).astype(BF)
+        dq = dot_tn(stacked(grads), stacked(per_head(mk_ref[there, :])))
         lanes = pl.ds(pl.multiple_of(step * GROUP, GROUP), GROUP)
         dq_ref[here, lanes] = (dq * SCALE).astype(BF)
-        dk_ref[there, :] = dot_nn(beside(grads), stacked(per_head(q))).astype(BF)
-        dv_ref[there, :] = dot_nn(beside(probs), stacked(per_head(mg))).astype(BF)
     acc_ref[...] += dot_nt(
         beside([dk_ref[...], dv_ref[...]]), beside([wk_ref[...], wv_ref[...]])
     )
@@ -362,14 +370,22 @@
     dpk = jnp.zeros((PREFIX_PAD, GROUP), F32)
     dpv = jnp.zeros((PREFIX_PAD, GROUP), F32)
     split = heads * PREFIX_PAD
+    raw = []
+    for s in range(seqs):
+        here = pl.ds(s * tgt, tgt)
+        raw.append(
+            (
+                dot_nt(stacked(pk + per_head(k_ref[here, :])), q_ref[here, :] * SCALE),
+                dot_nt(stacked(pv + per_head(v_ref[here, :])), ag_all[s * tgt : (s + 1) * tgt]),
+            )
+        )
     for s in range(seqs):
         bias = jnp.where((col <= row) & (col < len_ref[s]), 0.0, NEGATIVE)
         here = pl.ds(s * tgt, tgt)
         q = q_ref[here, :] * SCALE
         ag = ag_all[s * tgt : (s + 1) * tgt]
         keys = stacked(pk + per_head(k_ref[here, :]))
-        scores = dot_nt(keys, q)
-        dprobs = dot_nt(stacked(pv + per_head(v_ref[here, :])), ag)
+        scores, dprobs = raw[s]
         probs, grads = [], []
         for x, d, y, e in zip(
             cut(scores[split:], heads, 0),

time: 268 us -> 265 us (0.989)
  Pallas kernels: 119 us -> 116 us
    pallas_call x5, Pallas kernels: 111 us -> 108 us  [call(): pl.pallas_call(kernel, grid_spec=pltpu.PrefetchScalarGridSpec(num_scalar_...]
  transfers between devices with their start and end apart: 18 -> 18, of which waited for: 8 -> 8; matrix products, arithmetic and copies ran while one was open for 10% -> 10% of each run, Pallas kernels for 24% -> 23%
where the time goes in v1:
time: 265 us; the launch traced here: 264 us
  Pallas kernels  116 us (44%)
  waiting for transfers between devices  51 us (19%)
  starting transfers between devices  33.4 us (13%)
  local copies, waits for them, and re-layouts  32.7 us (12%)
  between operations  14.4 us (5%)
  blocking collectives  11.2 us (4%)
  other arithmetic  5.15 us (2%)
    pallas_call x5, Pallas kernels, call(): pl.pallas_call(kernel, grid_spec=pltpu.PrefetchScalarGridSpec(num_scalar_...  108 us
    all_gather x1, waiting for transfers between devices, local(): lax.all_gather(jnp.concatenate([jnp.moveaxis(spread, 0, 1).reshape(high,...  29.2 us
    dynamic_update_slice x10, local copies, waits for them, and re-layouts, ring_gather(): filled = lax.dynamic_update_slice_in_dim(filled, part, at, 0)  16.3 us
    all_gather x1, blocking collectives, local(): norms = lax.all_gather(vectors, DP, axis=1, tiled=True).astype(F32)  11.2 us
    ppermute x1, waiting for transfers between devices, ring_gather(): below = lax.ppermute(shard, 'dp_0', around(count, 1))  10.1 us
    pallas_call x1, Pallas kernels, input_gradient(): pl.pallas_call(input_grad_kernel, grid=(width // GROUP,), in_specs=[pl.Bl...  8.33 us
    all_to_all x1, starting transfers between devices, local(): lax.all_to_all(memory, MEM, split_axis=0, concat_axis=1, tiled=True)  8.13 us
    all_to_all x1, starting transfers between devices, local(): lax.all_to_all(joined.reshape(mem_groups, -1, joined.shape[1]), MEM, spli...  7.21 us
  transfers between devices with their start and end apart: 18, of which 8 were waited for; matrix products, arithmetic and copies ran while one was open for 10% of the time, Pallas kernels for 23%

profile of v1, /device:TPU:0, one launch (start us, length us, event | category | flops | bytes accessed | tf_op | source)
XLA Modules:
  0.0 263.8 jit_solution(6969627271590590954)
XLA Ops:
  7.3 0.0 all-gather.2.cloned.1.call-start
  7.3 1.1 copy-done
  8.5 0.9 dynamic-slice_dynamic-update-slice_fusion
  9.3 0.7 dynamic-slice_dynamic-update-slice_fusion.4
  10.1 0.7 dynamic-slice_dynamic-update-slice_fusion.3
  10.8 0.7 dynamic-slice_dynamic-update-slice_fusion.2
  11.5 0.8 dynamic-slice_dynamic-update-slice_fusion.1
  12.3 0.7 copy-done.3
  13.0 1.6 collective-permute-start.1
  14.6 1.7 collective-permute-start.3
  16.3 8.1 %all-to-all-start = ((bf16[32,24,1024]{2,1,0:T(8,128)(2,1)}), bf16[32,24,1024]{2,1,0:T(8,128)(2,1)S(1)}, u32[]{:S(2)}, u32[]{:S(2)}) async-start(bf16[32,24,1024]{2,1,0:T(8,128)(2,1)} %param.25), calls=%async_computation | async-start | bytes 3145728 | tf_op jit(solution)/shard_map/all_to_all | solution.py:724
  24.4 0.0 reduce-scatter.2.cloned.1.call-start
  24.5 10.1 %collective-permute-done.1 = bf16[128,3072]{1,0:T(8,128)(2,1)S(1)} collective-permute-done((bf16[128,3072]{1,0:T(8,128)(2,1)}, bf16[128,3072]{1,0:T(8,128)(2,1)S(1)}, u32[]{:S(2)}, u32[]{:S(2)}) %collective-permute-start.1) | collective-permute-done | bytes 786464 | tf_op jit(solution)/shard_map/ppermute | solution.py:667
  34.6 3.4 %broadcast_in_dim.13 = bf16[1024,3072]{1,0:T(8,128)(2,1)} broadcast(bf16[]{:T(256)} %constant.88.clone.1), dimensions={} | broadcast | bytes 6291458 | tf_op jit(solution)/shard_map/broadcast_in_dim | solution.py:669
  38.0 1.0 constant_dynamic-update-slice_fusion.10
  39.0 0.6 pad.11.pk_ref
  39.6 0.6 pad.12.pv_ref
  40.2 0.6 broadcast_in_dim.19
  40.8 0.6 broadcast_in_dim.18
  41.4 0.6 dynamic_slice.41.len_ref
  42.1 0.7 collective-permute-start.5
  42.8 2.7 %collective-permute-start.7 = (bf16[64,3072]{1,0:T(8,128)(2,1)S(1)}, bf16[64,3072]{1,0:T(8,128)(2,1)}, u32[]{:S(2)}, u32[]{:S(2)}) collective-permute-start(bf16[64,3072]{1,0:T(8,128)(2,1)S(1)} %slice.37), channel_id=1, source_target_pairs={{0,96},{32,0},{64,32},{96,64},{1,97},{33,1},{65,33},{97,65},{2,98}... | collective-permute-start | bytes 1179656 | tf_op jit(solution)/shard_map/ppermute | solution.py:672
  45.5 2.1 constant_dynamic-update-slice_fusion.9
  47.6 1.0 constant_dynamic-update-slice_fusion.8
  48.5 6.8 %collective-permute-done.5 = bf16[64,3072]{1,0:T(8,128)(2,1)} collective-permute-done((bf16[64,3072]{1,0:T(8,128)(2,1)S(1)}, bf16[64,3072]{1,0:T(8,128)(2,1)}, u32[]{:S(2)}, u32[]{:S(2)}) %collective-permute-start.5) | collective-permute-done | bytes 393248 | tf_op jit(solution)/shard_map/ppermute | solution.py:671
  55.4 0.5 collective-permute-start.8
  55.9 1.3 copy.34
  57.2 2.1 constant_dynamic-update-slice_fusion.7
  59.3 1.0 constant_dynamic-update-slice_fusion.6
  60.2 2.1 constant_dynamic-update-slice_fusion.5
  62.3 1.8 constant_dynamic-update-slice_fusion.4
  64.1 1.8 constant_dynamic-update-slice_fusion.3
  65.9 1.8 constant_dynamic-update-slice_fusion.2
  67.7 1.8 constant_dynamic-update-slice_fusion.1.wq_ref.wk_ref.wv_ref
  69.5 12.7 %shard_map.295 = (bf16[512,1024]{1,0:T(8,128)(2,1)}, bf16[512,1024]{1,0:T(8,128)(2,1)}, bf16[512,1024]{1,0:T(8,128)(2,1)}, bf16[512,1024]{1,0:T(8,128)(2,1)}) custom-call(s32[2]{0:T(128)} %len_ref.5, bf16[512,1024]{1,0:T(8,128)(2,1)} %bitcast.49, bf16[1024,3072]{1,0:T(8,128)(2,1)} %constant_dynamic-update-slice_fusion.1.wq_ref.wk_ref.wv_ref, ...), custom_call_target="tpu_custom_call" | custom-call | flops 3221225472 | bytes 14680064 | tf_op jit(solution)/shard_map/pallas_call | solution.py:457
  82.2 11.2 %all_gather.7 = bf16[8,1024]{1,0:T(8,128)(2,1)S(1)} all-gather(bf16[8,128]{1,0:T(8,128)(2,1)S(1)} %stack.29), channel_id=1, replica_groups=mesh['dp_0'=4,'dp_1'=2,'mem_0'=4,'mem_1'=4] {'dp_0','dp_1'}, dimensions={1}, use_global_device_ids=true | all-gather | bytes 18432 | tf_op jit(solution)/shard_map/all_gather | solution.py:739
  93.4 0.6 convert_element_type.25.norm_ref
  94.0 29.2 %all-gather.2.cloned.1.call-done.wk_ref.wv_ref.wo_ref.wcq_ref.wco_ref.win_ref.wff_ref.late_ref = bf16[1024,13312]{1,0:T(8,128)(2,1)} async-done(((bf16[8,13312]{1,0:T(8,128)(2,1)}), bf16[1024,13312]{1,0:T(8,128)(2,1)}) %all-gather.2.cloned.1.call-update) | async-done | bytes 27262992 | tf_op jit(solution)/shard_map/all_gather | solution.py:715
  123.2 18.7 %shard_map.296 = (bf16[768,1024]{1,0:T(8,128)(2,1)}, bf16[768,1024]{1,0:T(8,128)(2,1)}, bf16[512,1024]{1,0:T(8,128)(2,1)}, f32[512,1024]{1,0:T(8,128)}, f32[512,1]{1,0:T(8,128)}, /*index=5*/bf16[512,1024]{1,0:T(8,128)(2,1)}) custom-call(s32[2]{0:T(128)} %dynamic_slice.41.len_ref, bf16[768,1024]{1,0:T(8,128)(2,1)} %bitcast.48, ...), custom_call_target="tpu_custom_call" | custom-call | flops 5368709120 | bytes 16777216 | tf_op jit(solution)/shard_map/pallas_call | solution.py:457
  141.9 35.9 %shard_map.297 = (bf16[512,1024]{1,0:T(8,128)(2,1)}, f32[512,1024]{1,0:T(8,128)}, bf16[1024,1152]{1,0:T(8,128)(2,1)}) custom-call(s32[2]{0:T(128)} %len_ref.5, f32[512,1024]{1,0:T(8,128)} %get-tuple-element.41.nrm1_ref, bf16[512,1024]{1,0:T(8,128)(2,1)} %get-tuple-element.42.att_ref, ...), custom_call_target="tpu_custom_call" | custom-call | flops 20401094656 | bytes 33554432 | tf_op jit(solution)/shard_map/pallas_call | solution.py:457
  177.8 0.0 reduce-scatter.2.cloned.1.call-update
  177.8 25.5 %shard_map.298 = (bf16[16,2,24,1024]{3,2,1,0:T(8,128)(2,1)}, f32[512,1024]{1,0:T(8,128)}, bf16[512,1024]{1,0:T(8,128)(2,1)}) custom-call(s32[2]{0:T(128)} %dynamic_slice.41.len_ref, f32[512,1024]{1,0:T(8,128)} %get-tuple-element.44.gtwo_ref, bf16[1024,13312]{1,0:T(8,128)(2,1)} %all-gather.2.cloned.1.call-done.wk_ref.wv_ref.wo_ref.wcq_ref.wco_ref.win_ref.wff_ref.late_ref, ...), custom_call_target="tpu_custom_call" | custom-call | flops 4294967296 | bytes 14680064 | tf_op jit(solution)/shard_map/pallas_call | solution.py:457
  203.3 6.0 %all-to-all-start.1 = ((bf16[16,2,24,1024]{3,2,1,0:T(8,128)(2,1)}), bf16[16,2,24,1024]{3,2,1,0:T(8,128)(2,1)S(1)}, u32[]{:S(2)}, u32[]{:S(2)}) async-start(bf16[16,2,24,1024]{3,2,1,0:T(8,128)(2,1)} %get-tuple-element.56), calls=%async_computation.1 | async-start | bytes 3145728 | tf_op jit(solution)/shard_map/all_to_all | solution.py:750
  209.3 14.8 %shard_map.299 = (bf16[512,1024]{1,0:T(8,128)(2,1)}, bf16[512,1024]{1,0:T(8,128)(2,1)}, bf16[512,1024]{1,0:T(8,128)(2,1)}, f32[1024,128]{1,0:T(8,128)}) custom-call(s32[2]{0:T(128)} %len_ref.5, bf16[512,1024]{1,0:T(8,128)(2,1)} %get-tuple-element.50.low_ref, ...), custom_call_target="tpu_custom_call" | custom-call | flops 4294967296 | bytes 20971520 | tf_op jit(solution)/shard_map/pallas_call | solution.py:457
  224.0 1.0 dynamic-slice_bitcast_fusion
  225.0 0.1 collective-permute-start.9
  225.1 1.5 collective-permute-done.9
  226.6 1.0 bitcast_add_fusion
  227.6 0.6 collective-permute-start.10
  228.3 2.7 %collective-permute-start.11 = (f32[128,128]{1,0:T(8,128)S(1)}, f32[128,128]{1,0:T(8,128)S(1)}, u32[]{:S(2)}, u32[]{:S(2)}) collective-permute-start(f32[128,128]{1,0:T(8,128)S(1)} %get-tuple-element.67), channel_id=1, source_target_pairs={{0,64},{32,96},{64,0},{96,32},{1,65},{33,97},{65,1},{97,33},{2,66}... | collective-permute-start | bytes 196616 | tf_op jit(solution)/shard_map/ppermute | solution.py:694
  231.0 1.5 collective-permute-start.12
  232.4 1.4 collective-permute-done.10
  233.8 0.7 collective-permute-done.11
  234.5 0.8 collective-permute-done.12
  235.3 0.0 reduce-scatter.2.cloned.1.call-done
  235.3 1.7 fusion
  237.0 7.2 %all-to-all-start.2 = ((bf16[16,8,1152]{2,1,0:T(8,128)(2,1)}), bf16[16,8,1152]{2,1,0:T(8,128)(2,1)S(1)}, u32[]{:S(2)}, u32[]{:S(2)}) async-start(bf16[16,8,1152]{2,1,0:T(8,128)(2,1)} %fusion), calls=%async_computation.3 | async-start | bytes 589824 | tf_op jit(solution)/shard_map/all_to_all | solution.py:757
  244.2 8.3 %shard_map.300 = bf16[512,1024]{1,0:T(8,128)(2,1)} custom-call(f32[512,1024]{1,0:T(8,128)} %get-tuple-element.49.gone_ref, bf16[512,1024]{1,0:T(8,128)(2,1)} %get-tuple-element.57.dq_ref, bf16[512,1024]{1,0:T(8,128)(2,1)} %get-tuple-element.58.dk_ref, bf16[512,1024]{1,0:T(8,128)(2,1)} %get-tuple-element.59.dv_ref, ...), custom_call_target="tpu_custom_call" | custom-call | flops 3221225472 | bytes 12582912 | tf_op jit(solution)/shard_map/pallas_call | solution.py:641
  252.6 0.5 all-to-all-done.2
  253.1 0.7 slice_bitcast_fusion
  253.8 0.7 slice_reduce_fusion
  254.5 0.7 slice_reduce_fusion.1
  255.1 0.6 convert_reduce_fusion
  255.8 1.1 copy.51
  (50 shorter events, 0.3 us)
Async XLA Ops:
  7.2 1.2 copy-start
  7.2 31.8 %copy-start.4 = (bf16[30,1024]{1,0:T(8,128)(2,1)S(1)}, bf16[30,1024]{1,0:T(8,128)(2,1)}, u32[]{:S(2)}) copy-start(bf16[30,1024]{1,0:T(8,128)(2,1)} %param.42) | copy-start | bytes 184324
  7.2 32.4 %copy-start.5 = (bf16[30,1024]{1,0:T(8,128)(2,1)S(1)}, bf16[30,1024]{1,0:T(8,128)(2,1)}, u32[]{:S(2)}) copy-start(bf16[30,1024]{1,0:T(8,128)(2,1)} %param.43) | copy-start | bytes 184324
  7.2 33.0 %copy-start.7 = (bf16[1024]{0:T(1024)(128)(2,1)S(1)}, bf16[1024]{0:T(1024)(128)(2,1)}, u32[]{:S(2)}) copy-start(bf16[1024]{0:T(1024)(128)(2,1)} %param.47) | copy-start | bytes 6148
  7.2 33.6 %copy-start.8 = (bf16[512]{0:T(512)(128)(2,1)S(1)}, bf16[512]{0:T(512)(128)(2,1)}, u32[]{:S(2)}) copy-start(bf16[512]{0:T(512)(128)(2,1)} %param.45) | copy-start | bytes 3076
  7.2 34.7 %copy-start.6 = (bf16[128]{0:T(256)(128)(2,1)S(1)}, bf16[128]{0:T(256)(128)(2,1)}, u32[]{:S(2)}) copy-start(bf16[128]{0:T(256)(128)(2,1)} %param.41) | copy-start | bytes 772
  7.2 34.7 %copy-start.9 = (bf16[128]{0:T(256)(128)(2,1)S(1)}, bf16[128]{0:T(256)(128)(2,1)}, u32[]{:S(2)}) copy-start(bf16[128]{0:T(256)(128)(2,1)} %param.36) | copy-start | bytes 772
  7.3 116.0 %all-gather.2.cloned.1.call-start = ((), (), s32[]{:S(2)}) async-start(), calls=%async_computation.4 | async-start | bytes 27475968 | tf_op jit(solution)/shard_map/all_gather | solution.py:715
  8.4 33.0 %copy-start.14 = (s32[32]{0:T(128)S(1)}, s32[32]{0:T(128)}, u32[]{:S(2)}) copy-start(s32[32]{0:T(128)} %param.28) | copy-start | bytes 388
  8.4 33.6 %copy-start.10 = (bf16[128]{0:T(256)(128)(2,1)S(1)}, bf16[128]{0:T(256)(128)(2,1)}, u32[]{:S(2)}) copy-start(bf16[128]{0:T(256)(128)(2,1)} %param.37) | copy-start | bytes 772
  8.4 33.6 %copy-start.11 = (bf16[128]{0:T(256)(128)(2,1)S(1)}, bf16[128]{0:T(256)(128)(2,1)}, u32[]{:S(2)}) copy-start(bf16[128]{0:T(256)(128)(2,1)} %param.38) | copy-start | bytes 772
  8.4 33.6 %copy-start.12 = (bf16[128]{0:T(256)(128)(2,1)S(1)}, bf16[128]{0:T(256)(128)(2,1)}, u32[]{:S(2)}) copy-start(bf16[128]{0:T(256)(128)(2,1)} %param.39) | copy-start | bytes 772
  8.5 33.6 %copy-start.13 = (bf16[128]{0:T(256)(128)(2,1)S(1)}, bf16[128]{0:T(256)(128)(2,1)}, u32[]{:S(2)}) copy-start(bf16[128]{0:T(256)(128)(2,1)} %param.40) | copy-start | bytes 772
  12.3 0.7 copy-start.3
  13.0 21.6 %collective-permute-start.1 = (bf16[128,3072]{1,0:T(8,128)(2,1)}, bf16[128,3072]{1,0:T(8,128)(2,1)S(1)}, u32[]{:S(2)}, u32[]{:S(2)}) collective-permute-start(bf16[128,3072]{1,0:T(8,128)(2,1)} %param.29), channel_id=1, source_target_pairs={{0,32},{32,64},{64,96},{96,0},{1,33},{33,65},{65,97},{97,1},{2,34}... | collective-permute-start | bytes 2359304 | tf_op jit(solution)/shard_map/ppermute | solution.py:667
  14.6 28.1 %collective-permute-start.3 = (bf16[128,3072]{1,0:T(8,128)(2,1)}, bf16[128,3072]{1,0:T(8,128)(2,1)S(1)}, u32[]{:S(2)}, u32[]{:S(2)}) collective-permute-start(bf16[128,3072]{1,0:T(8,128)(2,1)} %param.29), channel_id=1, source_target_pairs={{0,96},{32,0},{64,32},{96,64},{1,97},{33,1},{65,33},{97,65},{2,98}... | collective-permute-start | bytes 2359304 | tf_op jit(solution)/shard_map/ppermute | solution.py:668
  16.3 29.2 %collective-permute-start = (bf16[128,3072]{1,0:T(8,128)(2,1)}, bf16[128,3072]{1,0:T(8,128)(2,1)}, u32[]{:S(2)}, u32[]{:S(2)}) collective-permute-start(bf16[128,3072]{1,0:T(8,128)(2,1)} %param.29), channel_id=1, source_target_pairs={{0,16},{16,0},{1,17},{17,1},{2,18},{18,2},{3,19},{19,3},{4,20},{20... | collective-permute-start | bytes 2359304 | tf_op jit(solution)/shard_map/ppermute | solution.py:676
  16.3 39.6 %all-to-all-start = ((bf16[32,24,1024]{2,1,0:T(8,128)(2,1)}), bf16[32,24,1024]{2,1,0:T(8,128)(2,1)S(1)}, u32[]{:S(2)}, u32[]{:S(2)}) async-start(bf16[32,24,1024]{2,1,0:T(8,128)(2,1)} %param.25), calls=%async_computation | async-start | bytes 3145728 | tf_op jit(solution)/shard_map/all_to_all | solution.py:724
  24.4 210.9 %reduce-scatter.2.cloned.1.call-start = ((), (), s32[]{:S(2)}) async-start(), calls=%async_computation.5 | async-start | bytes 2654208 | tf_op jit(solution)/shard_map/reduce_scatter | solution.py:745
  24.5 13.5 %copy-start.2 = (bf16[128,3072]{1,0:T(8,128)(2,1)S(1)}, bf16[128,3072]{1,0:T(8,128)(2,1)}, u32[]{:S(2)}) copy-start(bf16[128,3072]{1,0:T(8,128)(2,1)} %param.29) | copy-start | bytes 2359300
  34.6 22.6 %collective-permute-start.2 = (bf16[128,3072]{1,0:T(8,128)(2,1)S(1)}, bf16[128,3072]{1,0:T(8,128)(2,1)}, u32[]{:S(2)}, u32[]{:S(2)}) collective-permute-start(bf16[128,3072]{1,0:T(8,128)(2,1)S(1)} %collective-permute-done.1), channel_id=1, source_target_pairs={{0,16},{16,0},{1,17},{17,1},{2,18},{18,2},{3,19},{19,3},{4,20},{20... | collective-permute-start | bytes 2359304 | tf_op jit(solution)/shard_map/ppermute | solution.py:676
  42.1 13.3 %collective-permute-start.5 = (bf16[64,3072]{1,0:T(8,128)(2,1)S(1)}, bf16[64,3072]{1,0:T(8,128)(2,1)}, u32[]{:S(2)}, u32[]{:S(2)}) collective-permute-start(bf16[64,3072]{1,0:T(8,128)(2,1)S(1)} %slice.36), channel_id=1, source_target_pairs={{0,32},{32,64},{64,96},{96,0},{1,33},{33,65},{65,97},{97,1},{2,34}... | collective-permute-start | bytes 1179656 | tf_op jit(solution)/shard_map/ppermute | solution.py:671
  42.8 12.6 %collective-permute-start.7 = (bf16[64,3072]{1,0:T(8,128)(2,1)S(1)}, bf16[64,3072]{1,0:T(8,128)(2,1)}, u32[]{:S(2)}, u32[]{:S(2)}) collective-permute-start(bf16[64,3072]{1,0:T(8,128)(2,1)S(1)} %slice.37), channel_id=1, source_target_pairs={{0,96},{32,0},{64,32},{96,64},{1,97},{33,1},{65,33},{97,65},{2,98}... | collective-permute-start | bytes 1179656 | tf_op jit(solution)/shard_map/ppermute | solution.py:672
  45.5 14.8 %collective-permute-start.4 = (bf16[128,3072]{1,0:T(8,128)(2,1)S(1)}, bf16[128,3072]{1,0:T(8,128)(2,1)}, u32[]{:S(2)}, u32[]{:S(2)}) collective-permute-start(bf16[128,3072]{1,0:T(8,128)(2,1)S(1)} %collective-permute-done.3), channel_id=1, source_target_pairs={{0,16},{16,0},{1,17},{17,1},{2,18},{18,2},{3,19},{19,3},{4,20},{20... | collective-permute-start | bytes 2359304 | tf_op jit(solution)/shard_map/ppermute | solution.py:676
  55.4 8.8 %collective-permute-start.6 = (bf16[64,3072]{1,0:T(8,128)(2,1)}, bf16[64,3072]{1,0:T(8,128)(2,1)}, u32[]{:S(2)}, u32[]{:S(2)}) collective-permute-start(bf16[64,3072]{1,0:T(8,128)(2,1)} %collective-permute-done.5), channel_id=1, source_target_pairs={{0,16},{16,0},{1,17},{17,1},{2,18},{18,2},{3,19},{19,3},{4,20},{20... | collective-permute-start | bytes 1179656 | tf_op jit(solution)/shard_map/ppermute | solution.py:676
  55.4 12.3 %collective-permute-start.8 = (bf16[64,3072]{1,0:T(8,128)(2,1)}, bf16[64,3072]{1,0:T(8,128)(2,1)}, u32[]{:S(2)}, u32[]{:S(2)}) collective-permute-start(bf16[64,3072]{1,0:T(8,128)(2,1)} %collective-permute-done.7), channel_id=1, source_target_pairs={{0,16},{16,0},{1,17},{17,1},{2,18},{18,2},{3,19},{19,3},{4,20},{20... | collective-permute-start | bytes 1179656 | tf_op jit(solution)/shard_map/ppermute | solution.py:676
  203.3 31.9 %all-to-all-start.1 = ((bf16[16,2,24,1024]{3,2,1,0:T(8,128)(2,1)}), bf16[16,2,24,1024]{3,2,1,0:T(8,128)(2,1)S(1)}, u32[]{:S(2)}, u32[]{:S(2)}) async-start(bf16[16,2,24,1024]{3,2,1,0:T(8,128)(2,1)} %get-tuple-element.56), calls=%async_computation.1 | async-start | bytes 3145728 | tf_op jit(solution)/shard_map/all_to_all | solution.py:750
  225.0 1.6 collective-permute-start.9
  227.6 6.1 %collective-permute-start.10 = (f32[128,128]{1,0:T(8,128)S(1)}, f32[128,128]{1,0:T(8,128)S(1)}, u32[]{:S(2)}, u32[]{:S(2)}) collective-permute-start(f32[128,128]{1,0:T(8,128)S(1)} %get-tuple-element.65), channel_id=1, source_target_pairs={{0,32},{32,64},{64,96},{96,0},{1,33},{33,65},{65,97},{97,1},{2,34}... | collective-permute-start | bytes 196616 | tf_op jit(solution)/shard_map/ppermute | solution.py:694
  228.3 6.2 %collective-permute-start.11 = (f32[128,128]{1,0:T(8,128)S(1)}, f32[128,128]{1,0:T(8,128)S(1)}, u32[]{:S(2)}, u32[]{:S(2)}) collective-permute-start(f32[128,128]{1,0:T(8,128)S(1)} %get-tuple-element.67), channel_id=1, source_target_pairs={{0,64},{32,96},{64,0},{96,32},{1,65},{33,97},{65,1},{97,33},{2,66}... | collective-permute-start | bytes 196616 | tf_op jit(solution)/shard_map/ppermute | solution.py:694
  231.0 4.3 %collective-permute-start.12 = (f32[128,128]{1,0:T(8,128)S(1)}, f32[128,128]{1,0:T(8,128)S(1)}, u32[]{:S(2)}, u32[]{:S(2)}) collective-permute-start(f32[128,128]{1,0:T(8,128)S(1)} %get-tuple-element.66), channel_id=1, source_target_pairs={{0,96},{32,0},{64,32},{96,64},{1,97},{33,1},{65,33},{97,65},{2,98}... | collective-permute-start | bytes 196616 | tf_op jit(solution)/shard_map/ppermute | solution.py:694
  237.0 16.1 %all-to-all-start.2 = ((bf16[16,8,1152]{2,1,0:T(8,128)(2,1)}), bf16[16,8,1152]{2,1,0:T(8,128)(2,1)S(1)}, u32[]{:S(2)}, u32[]{:S(2)}) async-start(bf16[16,8,1152]{2,1,0:T(8,128)(2,1)} %fusion), calls=%async_computation.3 | async-start | bytes 589824 | tf_op jit(solution)/shard_map/all_to_all | solution.py:757
  244.2 12.7 %copy-start.1 = (bf16[512,1024]{1,0:T(8,128)(2,1)S(1)}, bf16[512,1024]{1,0:T(8,128)(2,1)}, u32[]{:S(2)}) copy-start(bf16[512,1024]{1,0:T(8,128)(2,1)} %param.35) | copy-start | bytes 3145732
Sparse Core Ops, SparseCore 0:
  13.1 110.0 all-gather.1
  177.9 33.4 reduce-scatter.1

commit v2 on v1

--- a/solution.py
+++ b/solution.py
@@ -420,7 +420,15 @@
         small_ref[at, :] = both.T
 
 
-def input_grad_kernel(gone_ref, dq_ref, dk_ref, dv_ref, wq_ref, wk_ref, wv_ref, din_ref):
+def input_grad_kernel(
+    gone_ref, dq_ref, dk_ref, dv_ref, wq_ref, wk_ref, wv_ref, arrived_ref, din_ref, given_ref, sem
+):
+    handed_on = pltpu.make_async_copy(arrived_ref, given_ref, sem.at[0])
+
+    @pl.when(pl.program_id(0) == 0)
+    def _():
+        handed_on.start()
+
     din_ref[...] = (
         gone_ref[...]
         + dot_nt(
@@ -428,6 +436,10 @@
             beside([wq_ref[...], wk_ref[...], wv_ref[...]]),
         )
     ).astype(BF)
+
+    @pl.when(pl.program_id(0) == pl.num_programs(0) - 1)
+    def _():
+        handed_on.wait()
 
 
 ANYWHERE = pl.BlockSpec(memory_space=pl.ANY)
@@ -632,7 +644,7 @@
     )
 
 
-def input_gradient(gone, dq, dk, dv, early):
+def input_gradient(gone, dq, dk, dv, early, arrived):
     rows, width = gone.shape
 
     def part(index):
@@ -643,16 +655,17 @@
         grid=(width // GROUP,),
         in_specs=[pl.BlockSpec((rows, GROUP), lambda i: (0, i))]
         + [whole((rows, width))] * 3
-        + [part(0), part(1), part(2)],
-        out_specs=pl.BlockSpec((rows, GROUP), lambda i: (0, i)),
-        out_shape=shaped((rows, width), BF),
+        + [part(0), part(1), part(2), pl.BlockSpec(memory_space=pltpu.VMEM)],
+        out_specs=[pl.BlockSpec((rows, GROUP), lambda i: (0, i)), ANYWHERE],
+        out_shape=[shaped((rows, width), BF), shaped(arrived.shape, arrived.dtype)],
+        scratch_shapes=[pltpu.SemaphoreType.DMA((1,))],
         compiler_params=pltpu.CompilerParams(
             vmem_limit_bytes=VMEM_BYTES, dimension_semantics=("arbitrary",)
         ),
         cost_estimate=pl.CostEstimate(
             flops=6 * rows * width * width, bytes_accessed=12 * width * width, transcendentals=0
         ),
-    )(gone, dq, dk, dv, early, early, early)
+    )(gone, dq, dk, dv, early, early, early, arrived)
 
 
 def around(count, by):
@@ -751,7 +764,8 @@
     dq, dk, dv, small = self_backward(tgt_len, gone_low, late, q, k, v, pk, pv)
     small = scatter_sum(small.reshape(lax.axis_size(DP), -1, PAIR))
     dq, small, memory_grad = lax.optimization_barrier((dq, small, memory_grad))
-    din = input_gradient(gone, dq, dk, dv, early)
+    memory_grad = memory_grad.reshape(memory.shape)
+    din, memory_grad = input_gradient(gone, dq, dk, dv, early, memory_grad)
     adapt = down_weight.shape[1]
     joined = (adapter.astype(F32) + jnp.pad(small, ((0, 0), (2 * adapt, 0)))).astype(BF)
     arrived = lax.all_to_all(
@@ -765,7 +779,7 @@
     return (
         output.reshape(tokens.shape),
         din.reshape(tokens.shape),
-        memory_grad.reshape(memory.shape),
+        memory_grad,
         last[:, :prefix].T,
         last[:, PREFIX_PAD : PREFIX_PAD + prefix].T,
         down_grad,

time: 265 us -> 264 us (level)
    unnamed x36 -> x37, local copies, waits for them, and re-layouts: 6.03 us -> 4.9 us
  transfers between devices with their start and end apart: 18 -> 18, of which waited for: 8 -> 7; matrix products, arithmetic and copies ran while one was open for 10% -> 10% of each run, Pallas kernels for 23% -> 23%
where the time goes in v2:
time: 264 us; the launch traced here: 263 us
  Pallas kernels  116 us (44%)
  waiting for transfers between devices  50.5 us (19%)
  starting transfers between devices  33.4 us (13%)
  local copies, waits for them, and re-layouts  31.6 us (12%)
  between operations  14.4 us (5%)
  blocking collectives  11.2 us (4%)
  other arithmetic  5.37 us (2%)
    pallas_call x5, Pallas kernels, call(): pl.pallas_call(kernel, grid_spec=pltpu.PrefetchScalarGridSpec(num_scalar_...  108 us
    all_gather x1, waiting for transfers between devices, local(): lax.all_gather(jnp.concatenate([jnp.moveaxis(spread, 0, 1).reshape(high,...  29.2 us
    dynamic_update_slice x10, local copies, waits for them, and re-layouts, ring_gather(): filled = lax.dynamic_update_slice_in_dim(filled, part, at, 0)  16.2 us
    all_gather x1, blocking collectives, local(): norms = lax.all_gather(vectors, DP, axis=1, tiled=True).astype(F32)  11.2 us
    ppermute x1, waiting for transfers between devices, ring_gather(): below = lax.ppermute(shard, 'dp_0', around(count, 1))  10.1 us
    pallas_call x1, Pallas kernels, input_gradient(): pl.pallas_call(input_grad_kernel, grid=(width // GROUP,), in_specs=[pl.Bl...  8.85 us
    all_to_all x1, starting transfers between devices, local(): lax.all_to_all(memory, MEM, split_axis=0, concat_axis=1, tiled=True)  8.13 us
    all_to_all x1, starting transfers between devices, local(): lax.all_to_all(joined.reshape(mem_groups, -1, joined.shape[1]), MEM, spli...  7.22 us
  transfers between devices with their start and end apart: 18, of which 7 were waited for; matrix products, arithmetic and copies ran while one was open for 10% of the time, Pallas kernels for 23%

profile of v2, /device:TPU:0, one launch (start us, length us, event | category | flops | bytes accessed | tf_op | source)
XLA Modules:
  0.0 262.9 jit_solution(15010980391345795556)
XLA Ops:
  7.2 0.0 copy-start
  7.3 0.0 all-gather.2.cloned.1.call-start
  7.3 1.1 copy-done
  8.5 0.9 dynamic-slice_dynamic-update-slice_fusion
  9.3 0.7 dynamic-slice_dynamic-update-slice_fusion.4
  10.1 0.7 dynamic-slice_dynamic-update-slice_fusion.3
  10.8 0.7 dynamic-slice_dynamic-update-slice_fusion.2
  11.5 0.8 dynamic-slice_dynamic-update-slice_fusion.1
  12.3 0.7 copy-done.4
  13.0 0.0 all-gather.2.cloned.1.call-update
  13.0 1.6 collective-permute-start.1
  14.6 1.7 collective-permute-start.3
  16.3 8.1 %all-to-all-start = ((bf16[32,24,1024]{2,1,0:T(8,128)(2,1)}), bf16[32,24,1024]{2,1,0:T(8,128)(2,1)S(1)}, u32[]{:S(2)}, u32[]{:S(2)}) async-start(bf16[32,24,1024]{2,1,0:T(8,128)(2,1)} %param.25), calls=%async_computation | async-start | bytes 3145728 | tf_op jit(solution)/shard_map/all_to_all | solution.py:737
  24.4 0.0 reduce-scatter.2.cloned.1.call-start
  24.5 10.1 %collective-permute-done.1 = bf16[128,3072]{1,0:T(8,128)(2,1)S(1)} collective-permute-done((bf16[128,3072]{1,0:T(8,128)(2,1)}, bf16[128,3072]{1,0:T(8,128)(2,1)S(1)}, u32[]{:S(2)}, u32[]{:S(2)}) %collective-permute-start.1) | collective-permute-done | bytes 786464 | tf_op jit(solution)/shard_map/ppermute | solution.py:680
  34.6 3.4 %broadcast_in_dim.13 = bf16[1024,3072]{1,0:T(8,128)(2,1)} broadcast(bf16[]{:T(256)} %constant.88.clone.1), dimensions={} | broadcast | bytes 6291458 | tf_op jit(solution)/shard_map/broadcast_in_dim | solution.py:682
  38.0 0.9 constant_dynamic-update-slice_fusion.10
  39.0 0.6 pad.11.pk_ref
  39.6 0.6 pad.12.pv_ref
  40.2 0.6 broadcast_in_dim.19
  40.8 0.6 broadcast_in_dim.18
  41.4 0.6 dynamic_slice.41.len_ref
  42.1 0.7 collective-permute-start.5
  42.8 2.7 %collective-permute-start.7 = (bf16[64,3072]{1,0:T(8,128)(2,1)S(1)}, bf16[64,3072]{1,0:T(8,128)(2,1)}, u32[]{:S(2)}, u32[]{:S(2)}) collective-permute-start(bf16[64,3072]{1,0:T(8,128)(2,1)S(1)} %slice.37), channel_id=1, source_target_pairs={{0,96},{32,0},{64,32},{96,64},{1,97},{33,1},{65,33},{97,65},{2,98}... | collective-permute-start | bytes 1179656 | tf_op jit(solution)/shard_map/ppermute | solution.py:685
  45.5 2.1 constant_dynamic-update-slice_fusion.9
  47.6 1.0 constant_dynamic-update-slice_fusion.8
  48.6 6.8 %collective-permute-done.5 = bf16[64,3072]{1,0:T(8,128)(2,1)} collective-permute-done((bf16[64,3072]{1,0:T(8,128)(2,1)S(1)}, bf16[64,3072]{1,0:T(8,128)(2,1)}, u32[]{:S(2)}, u32[]{:S(2)}) %collective-permute-start.5) | collective-permute-done | bytes 393248 | tf_op jit(solution)/shard_map/ppermute | solution.py:684
  55.4 0.5 collective-permute-start.8
  55.9 1.3 copy.34
  57.2 2.1 constant_dynamic-update-slice_fusion.7
  59.3 1.0 constant_dynamic-update-slice_fusion.6
  60.3 2.1 constant_dynamic-update-slice_fusion.5
  62.3 1.8 constant_dynamic-update-slice_fusion.4
  64.1 1.8 constant_dynamic-update-slice_fusion.3
  65.9 1.8 constant_dynamic-update-slice_fusion.2
  67.7 1.8 constant_dynamic-update-slice_fusion.1.wq_ref.wk_ref.wv_ref
  69.5 12.7 %shard_map.295 = (bf16[512,1024]{1,0:T(8,128)(2,1)}, bf16[512,1024]{1,0:T(8,128)(2,1)}, bf16[512,1024]{1,0:T(8,128)(2,1)}, bf16[512,1024]{1,0:T(8,128)(2,1)}) custom-call(s32[2]{0:T(128)} %len_ref.5, bf16[512,1024]{1,0:T(8,128)(2,1)} %bitcast.49, bf16[1024,3072]{1,0:T(8,128)(2,1)} %constant_dynamic-update-slice_fusion.1.wq_ref.wk_ref.wv_ref, ...), custom_call_target="tpu_custom_call" | custom-call | flops 3221225472 | bytes 14680064 | tf_op jit(solution)/shard_map/pallas_call | solution.py:469
  82.2 11.2 %all_gather.7 = bf16[8,1024]{1,0:T(8,128)(2,1)S(1)} all-gather(bf16[8,128]{1,0:T(8,128)(2,1)S(1)} %stack.29), channel_id=1, replica_groups=mesh['dp_0'=4,'dp_1'=2,'mem_0'=4,'mem_1'=4] {'dp_0','dp_1'}, dimensions={1}, use_global_device_ids=true | all-gather | bytes 18432 | tf_op jit(solution)/shard_map/all_gather | solution.py:752
  93.4 0.6 convert_element_type.25.norm_ref
  94.0 29.2 %all-gather.2.cloned.1.call-done.wk_ref.wv_ref.wo_ref.wcq_ref.wco_ref.win_ref.wff_ref.late_ref = bf16[1024,13312]{1,0:T(8,128)(2,1)} async-done(((bf16[8,13312]{1,0:T(8,128)(2,1)}), bf16[1024,13312]{1,0:T(8,128)(2,1)}) %all-gather.2.cloned.1.call-update) | async-done | bytes 27262992 | tf_op jit(solution)/shard_map/all_gather | solution.py:728
  123.2 18.7 %shard_map.296 = (bf16[768,1024]{1,0:T(8,128)(2,1)}, bf16[768,1024]{1,0:T(8,128)(2,1)}, bf16[512,1024]{1,0:T(8,128)(2,1)}, f32[512,1024]{1,0:T(8,128)}, f32[512,1]{1,0:T(8,128)}, /*index=5*/bf16[512,1024]{1,0:T(8,128)(2,1)}) custom-call(s32[2]{0:T(128)} %dynamic_slice.41.len_ref, bf16[768,1024]{1,0:T(8,128)(2,1)} %bitcast.48, ...), custom_call_target="tpu_custom_call" | custom-call | flops 5368709120 | bytes 16777216 | tf_op jit(solution)/shard_map/pallas_call | solution.py:469
  141.9 35.9 %shard_map.297 = (bf16[512,1024]{1,0:T(8,128)(2,1)}, f32[512,1024]{1,0:T(8,128)}, bf16[1024,1152]{1,0:T(8,128)(2,1)}) custom-call(s32[2]{0:T(128)} %len_ref.5, f32[512,1024]{1,0:T(8,128)} %get-tuple-element.43.nrm1_ref, bf16[512,1024]{1,0:T(8,128)(2,1)} %get-tuple-element.44.att_ref, ...), custom_call_target="tpu_custom_call" | custom-call | flops 20401094656 | bytes 33554432 | tf_op jit(solution)/shard_map/pallas_call | solution.py:469
  177.8 0.0 reduce-scatter.2.cloned.1.call-update
  177.8 25.5 %shard_map.298 = (bf16[16,2,24,1024]{3,2,1,0:T(8,128)(2,1)}, f32[512,1024]{1,0:T(8,128)}, bf16[512,1024]{1,0:T(8,128)(2,1)}) custom-call(s32[2]{0:T(128)} %dynamic_slice.41.len_ref, f32[512,1024]{1,0:T(8,128)} %get-tuple-element.46.gtwo_ref, bf16[1024,13312]{1,0:T(8,128)(2,1)} %all-gather.2.cloned.1.call-done.wk_ref.wv_ref.wo_ref.wcq_ref.wco_ref.win_ref.wff_ref.late_ref, ...), custom_call_target="tpu_custom_call" | custom-call | flops 4294967296 | bytes 14680064 | tf_op jit(solution)/shard_map/pallas_call | solution.py:469
  203.3 6.0 %all-to-all-start.1 = ((bf16[16,2,24,1024]{3,2,1,0:T(8,128)(2,1)}), bf16[16,2,24,1024]{3,2,1,0:T(8,128)(2,1)S(1)}, u32[]{:S(2)}, u32[]{:S(2)}) async-start(bf16[16,2,24,1024]{3,2,1,0:T(8,128)(2,1)} %get-tuple-element.58), calls=%async_computation.1 | async-start | bytes 3145728 | tf_op jit(solution)/shard_map/all_to_all | solution.py:763
  209.3 14.7 %shard_map.299 = (bf16[512,1024]{1,0:T(8,128)(2,1)}, bf16[512,1024]{1,0:T(8,128)(2,1)}, bf16[512,1024]{1,0:T(8,128)(2,1)}, f32[1024,128]{1,0:T(8,128)}) custom-call(s32[2]{0:T(128)} %len_ref.5, bf16[512,1024]{1,0:T(8,128)(2,1)} %get-tuple-element.52.low_ref, ...), custom_call_target="tpu_custom_call" | custom-call | flops 4294967296 | bytes 20971520 | tf_op jit(solution)/shard_map/pallas_call | solution.py:469
  224.0 1.0 dynamic-slice_bitcast_fusion
  225.0 0.1 collective-permute-start.9
  225.1 1.5 collective-permute-done.9
  226.6 1.0 bitcast_add_fusion
  227.6 0.6 collective-permute-start.10
  228.3 2.7 %collective-permute-start.11 = (f32[128,128]{1,0:T(8,128)S(1)}, f32[128,128]{1,0:T(8,128)S(1)}, u32[]{:S(2)}, u32[]{:S(2)}) collective-permute-start(f32[128,128]{1,0:T(8,128)S(1)} %get-tuple-element.71), channel_id=1, source_target_pairs={{0,64},{32,96},{64,0},{96,32},{1,65},{33,97},{65,1},{97,33},{2,66}... | collective-permute-start | bytes 196616 | tf_op jit(solution)/shard_map/ppermute | solution.py:707
  230.9 1.5 collective-permute-start.12
  232.4 1.3 collective-permute-done.10
  233.8 0.7 collective-permute-done.11
  234.5 0.8 collective-permute-done.12
  235.3 0.0 reduce-scatter.2.cloned.1.call-done
  235.3 1.9 fusion
  237.2 7.2 %all-to-all-start.2 = ((bf16[16,8,1152]{2,1,0:T(8,128)(2,1)}), bf16[16,8,1152]{2,1,0:T(8,128)(2,1)S(1)}, u32[]{:S(2)}, u32[]{:S(2)}) async-start(bf16[16,8,1152]{2,1,0:T(8,128)(2,1)} %fusion), calls=%async_computation.3 | async-start | bytes 589824 | tf_op jit(solution)/shard_map/all_to_all | solution.py:771
  244.5 8.8 %shard_map.300 = (bf16[512,1024]{1,0:T(8,128)(2,1)}, bf16[32,24,1024]{2,1,0:T(8,128)(2,1)}) custom-call(f32[512,1024]{1,0:T(8,128)} %get-tuple-element.51.gone_ref, bf16[512,1024]{1,0:T(8,128)(2,1)} %get-tuple-element.59.dq_ref, bf16[512,1024]{1,0:T(8,128)(2,1)} %get-tuple-element.60.dk_ref, bf16[512,1024]{1,0:T(8,128)(2,1)} %get-tuple-element.61.dv_ref, ...), custom_call_target="tpu_custom_call" | custom-call | flops 3221225472 | bytes 12582912 | tf_op jit(solution)/shard_map/pallas_call | solution.py:653
  253.3 0.7 slice_bitcast_fusion
  254.0 0.7 slice_reduce_fusion
  254.7 0.7 slice_reduce_fusion.1
  255.4 0.6 convert_reduce_fusion
  (51 shorter events, 0.3 us)
Async XLA Ops:
  7.2 1.2 copy-start
  7.2 31.8 %copy-start.5 = (bf16[30,1024]{1,0:T(8,128)(2,1)S(1)}, bf16[30,1024]{1,0:T(8,128)(2,1)}, u32[]{:S(2)}) copy-start(bf16[30,1024]{1,0:T(8,128)(2,1)} %param.42) | copy-start | bytes 184324
  7.2 32.4 %copy-start.6 = (bf16[30,1024]{1,0:T(8,128)(2,1)S(1)}, bf16[30,1024]{1,0:T(8,128)(2,1)}, u32[]{:S(2)}) copy-start(bf16[30,1024]{1,0:T(8,128)(2,1)} %param.43) | copy-start | bytes 184324
  7.2 33.0 %copy-start.8 = (bf16[1024]{0:T(1024)(128)(2,1)S(1)}, bf16[1024]{0:T(1024)(128)(2,1)}, u32[]{:S(2)}) copy-start(bf16[1024]{0:T(1024)(128)(2,1)} %param.47) | copy-start | bytes 6148
  7.2 33.6 %copy-start.9 = (bf16[512]{0:T(512)(128)(2,1)S(1)}, bf16[512]{0:T(512)(128)(2,1)}, u32[]{:S(2)}) copy-start(bf16[512]{0:T(512)(128)(2,1)} %param.45) | copy-start | bytes 3076
  7.2 34.8 %copy-start.7 = (bf16[128]{0:T(256)(128)(2,1)S(1)}, bf16[128]{0:T(256)(128)(2,1)}, u32[]{:S(2)}) copy-start(bf16[128]{0:T(256)(128)(2,1)} %param.41) | copy-start | bytes 772
  7.2 34.8 %copy-start.10 = (bf16[128]{0:T(256)(128)(2,1)S(1)}, bf16[128]{0:T(256)(128)(2,1)}, u32[]{:S(2)}) copy-start(bf16[128]{0:T(256)(128)(2,1)} %param.36) | copy-start | bytes 772
  7.3 116.0 %all-gather.2.cloned.1.call-start = ((), (), s32[]{:S(2)}) async-start(), calls=%async_computation.4 | async-start | bytes 27475968 | tf_op jit(solution)/shard_map/all_gather | solution.py:728
  8.4 33.0 %copy-start.15 = (s32[32]{0:T(128)S(1)}, s32[32]{0:T(128)}, u32[]{:S(2)}) copy-start(s32[32]{0:T(128)} %param.28) | copy-start | bytes 388
  8.4 33.6 %copy-start.11 = (bf16[128]{0:T(256)(128)(2,1)S(1)}, bf16[128]{0:T(256)(128)(2,1)}, u32[]{:S(2)}) copy-start(bf16[128]{0:T(256)(128)(2,1)} %param.37) | copy-start | bytes 772
  8.4 33.6 %copy-start.12 = (bf16[128]{0:T(256)(128)(2,1)S(1)}, bf16[128]{0:T(256)(128)(2,1)}, u32[]{:S(2)}) copy-start(bf16[128]{0:T(256)(128)(2,1)} %param.38) | copy-start | bytes 772
  8.4 33.6 %copy-start.13 = (bf16[128]{0:T(256)(128)(2,1)S(1)}, bf16[128]{0:T(256)(128)(2,1)}, u32[]{:S(2)}) copy-start(bf16[128]{0:T(256)(128)(2,1)} %param.39) | copy-start | bytes 772
  8.5 33.6 %copy-start.14 = (bf16[128]{0:T(256)(128)(2,1)S(1)}, bf16[128]{0:T(256)(128)(2,1)}, u32[]{:S(2)}) copy-start(bf16[128]{0:T(256)(128)(2,1)} %param.40) | copy-start | bytes 772
  12.3 0.7 copy-start.4
  13.0 21.6 %collective-permute-start.1 = (bf16[128,3072]{1,0:T(8,128)(2,1)}, bf16[128,3072]{1,0:T(8,128)(2,1)S(1)}, u32[]{:S(2)}, u32[]{:S(2)}) collective-permute-start(bf16[128,3072]{1,0:T(8,128)(2,1)} %param.29), channel_id=1, source_target_pairs={{0,32},{32,64},{64,96},{96,0},{1,33},{33,65},{65,97},{97,1},{2,34}... | collective-permute-start | bytes 2359304 | tf_op jit(solution)/shard_map/ppermute | solution.py:680
  14.6 28.1 %collective-permute-start.3 = (bf16[128,3072]{1,0:T(8,128)(2,1)}, bf16[128,3072]{1,0:T(8,128)(2,1)S(1)}, u32[]{:S(2)}, u32[]{:S(2)}) collective-permute-start(bf16[128,3072]{1,0:T(8,128)(2,1)} %param.29), channel_id=1, source_target_pairs={{0,96},{32,0},{64,32},{96,64},{1,97},{33,1},{65,33},{97,65},{2,98}... | collective-permute-start | bytes 2359304 | tf_op jit(solution)/shard_map/ppermute | solution.py:681
  16.3 29.2 %collective-permute-start = (bf16[128,3072]{1,0:T(8,128)(2,1)}, bf16[128,3072]{1,0:T(8,128)(2,1)}, u32[]{:S(2)}, u32[]{:S(2)}) collective-permute-start(bf16[128,3072]{1,0:T(8,128)(2,1)} %param.29), channel_id=1, source_target_pairs={{0,16},{16,0},{1,17},{17,1},{2,18},{18,2},{3,19},{19,3},{4,20},{20... | collective-permute-start | bytes 2359304 | tf_op jit(solution)/shard_map/ppermute | solution.py:689
  16.3 39.6 %all-to-all-start = ((bf16[32,24,1024]{2,1,0:T(8,128)(2,1)}), bf16[32,24,1024]{2,1,0:T(8,128)(2,1)S(1)}, u32[]{:S(2)}, u32[]{:S(2)}) async-start(bf16[32,24,1024]{2,1,0:T(8,128)(2,1)} %param.25), calls=%async_computation | async-start | bytes 3145728 | tf_op jit(solution)/shard_map/all_to_all | solution.py:737
  24.4 210.9 %reduce-scatter.2.cloned.1.call-start = ((), (), s32[]{:S(2)}) async-start(), calls=%async_computation.5 | async-start | bytes 2654208 | tf_op jit(solution)/shard_map/reduce_scatter | solution.py:758
  24.5 13.5 %copy-start.3 = (bf16[128,3072]{1,0:T(8,128)(2,1)S(1)}, bf16[128,3072]{1,0:T(8,128)(2,1)}, u32[]{:S(2)}) copy-start(bf16[128,3072]{1,0:T(8,128)(2,1)} %param.29) | copy-start | bytes 2359300
  34.6 22.6 %collective-permute-start.2 = (bf16[128,3072]{1,0:T(8,128)(2,1)S(1)}, bf16[128,3072]{1,0:T(8,128)(2,1)}, u32[]{:S(2)}, u32[]{:S(2)}) collective-permute-start(bf16[128,3072]{1,0:T(8,128)(2,1)S(1)} %collective-permute-done.1), channel_id=1, source_target_pairs={{0,16},{16,0},{1,17},{17,1},{2,18},{18,2},{3,19},{19,3},{4,20},{20... | collective-permute-start | bytes 2359304 | tf_op jit(solution)/shard_map/ppermute | solution.py:689
  42.1 13.3 %collective-permute-start.5 = (bf16[64,3072]{1,0:T(8,128)(2,1)S(1)}, bf16[64,3072]{1,0:T(8,128)(2,1)}, u32[]{:S(2)}, u32[]{:S(2)}) collective-permute-start(bf16[64,3072]{1,0:T(8,128)(2,1)S(1)} %slice.36), channel_id=1, source_target_pairs={{0,32},{32,64},{64,96},{96,0},{1,33},{33,65},{65,97},{97,1},{2,34}... | collective-permute-start | bytes 1179656 | tf_op jit(solution)/shard_map/ppermute | solution.py:684
  42.8 12.6 %collective-permute-start.7 = (bf16[64,3072]{1,0:T(8,128)(2,1)S(1)}, bf16[64,3072]{1,0:T(8,128)(2,1)}, u32[]{:S(2)}, u32[]{:S(2)}) collective-permute-start(bf16[64,3072]{1,0:T(8,128)(2,1)S(1)} %slice.37), channel_id=1, source_target_pairs={{0,96},{32,0},{64,32},{96,64},{1,97},{33,1},{65,33},{97,65},{2,98}... | collective-permute-start | bytes 1179656 | tf_op jit(solution)/shard_map/ppermute | solution.py:685
  45.5 14.8 %collective-permute-start.4 = (bf16[128,3072]{1,0:T(8,128)(2,1)S(1)}, bf16[128,3072]{1,0:T(8,128)(2,1)}, u32[]{:S(2)}, u32[]{:S(2)}) collective-permute-start(bf16[128,3072]{1,0:T(8,128)(2,1)S(1)} %collective-permute-done.3), channel_id=1, source_target_pairs={{0,16},{16,0},{1,17},{17,1},{2,18},{18,2},{3,19},{19,3},{4,20},{20... | collective-permute-start | bytes 2359304 | tf_op jit(solution)/shard_map/ppermute | solution.py:689
  55.4 8.7 %collective-permute-start.6 = (bf16[64,3072]{1,0:T(8,128)(2,1)}, bf16[64,3072]{1,0:T(8,128)(2,1)}, u32[]{:S(2)}, u32[]{:S(2)}) collective-permute-start(bf16[64,3072]{1,0:T(8,128)(2,1)} %collective-permute-done.5), channel_id=1, source_target_pairs={{0,16},{16,0},{1,17},{17,1},{2,18},{18,2},{3,19},{19,3},{4,20},{20... | collective-permute-start | bytes 1179656 | tf_op jit(solution)/shard_map/ppermute | solution.py:689
  55.4 12.3 %collective-permute-start.8 = (bf16[64,3072]{1,0:T(8,128)(2,1)}, bf16[64,3072]{1,0:T(8,128)(2,1)}, u32[]{:S(2)}, u32[]{:S(2)}) collective-permute-start(bf16[64,3072]{1,0:T(8,128)(2,1)} %collective-permute-done.7), channel_id=1, source_target_pairs={{0,16},{16,0},{1,17},{17,1},{2,18},{18,2},{3,19},{19,3},{4,20},{20... | collective-permute-start | bytes 1179656 | tf_op jit(solution)/shard_map/ppermute | solution.py:689
  203.3 31.9 %all-to-all-start.1 = ((bf16[16,2,24,1024]{3,2,1,0:T(8,128)(2,1)}), bf16[16,2,24,1024]{3,2,1,0:T(8,128)(2,1)S(1)}, u32[]{:S(2)}, u32[]{:S(2)}) async-start(bf16[16,2,24,1024]{3,2,1,0:T(8,128)(2,1)} %get-tuple-element.58), calls=%async_computation.1 | async-start | bytes 3145728 | tf_op jit(solution)/shard_map/all_to_all | solution.py:763
  225.0 1.6 collective-permute-start.9
  227.6 6.1 %collective-permute-start.10 = (f32[128,128]{1,0:T(8,128)S(1)}, f32[128,128]{1,0:T(8,128)S(1)}, u32[]{:S(2)}, u32[]{:S(2)}) collective-permute-start(f32[128,128]{1,0:T(8,128)S(1)} %get-tuple-element.69), channel_id=1, source_target_pairs={{0,32},{32,64},{64,96},{96,0},{1,33},{33,65},{65,97},{97,1},{2,34}... | collective-permute-start | bytes 196616 | tf_op jit(solution)/shard_map/ppermute | solution.py:707
  228.3 6.2 %collective-permute-start.11 = (f32[128,128]{1,0:T(8,128)S(1)}, f32[128,128]{1,0:T(8,128)S(1)}, u32[]{:S(2)}, u32[]{:S(2)}) collective-permute-start(f32[128,128]{1,0:T(8,128)S(1)} %get-tuple-element.71), channel_id=1, source_target_pairs={{0,64},{32,96},{64,0},{96,32},{1,65},{33,97},{65,1},{97,33},{2,66}... | collective-permute-start | bytes 196616 | tf_op jit(solution)/shard_map/ppermute | solution.py:707
  230.9 4.3 %collective-permute-start.12 = (f32[128,128]{1,0:T(8,128)S(1)}, f32[128,128]{1,0:T(8,128)S(1)}, u32[]{:S(2)}, u32[]{:S(2)}) collective-permute-start(f32[128,128]{1,0:T(8,128)S(1)} %get-tuple-element.70), channel_id=1, source_target_pairs={{0,96},{32,0},{64,32},{96,64},{1,97},{33,1},{65,33},{97,65},{2,98}... | collective-permute-start | bytes 196616 | tf_op jit(solution)/shard_map/ppermute | solution.py:707
  235.3 9.2 %copy-start.2 = (bf16[16,2,24,1024]{3,2,1,0:T(8,128)(2,1)}, bf16[16,2,24,1024]{3,2,1,0:T(8,128)(2,1)S(1)}, u32[]{:S(2)}) copy-start(bf16[16,2,24,1024]{3,2,1,0:T(8,128)(2,1)S(1)} %all-to-all-done.1) | copy-start | bytes 4718596
  237.2 16.1 %all-to-all-start.2 = ((bf16[16,8,1152]{2,1,0:T(8,128)(2,1)}), bf16[16,8,1152]{2,1,0:T(8,128)(2,1)S(1)}, u32[]{:S(2)}, u32[]{:S(2)}) async-start(bf16[16,8,1152]{2,1,0:T(8,128)(2,1)} %fusion), calls=%async_computation.3 | async-start | bytes 589824 | tf_op jit(solution)/shard_map/all_to_all | solution.py:771
  244.4 11.6 %copy-start.1 = (bf16[512,1024]{1,0:T(8,128)(2,1)S(1)}, bf16[512,1024]{1,0:T(8,128)(2,1)}, u32[]{:S(2)}) copy-start(bf16[512,1024]{1,0:T(8,128)(2,1)} %param.35) | copy-start | bytes 3145732
Sparse Core Ops, SparseCore 0:
  13.1 110.0 all-gather.1
  178.0 33.4 reduce-scatter.1
